TPU v7x, 32 devices: a whole 2x2x4 slice. The times are simulated.
32 devices in a mesh: ctx: 8 (over y, x, core), wsh: 4 (over z).
Axes of the slice: x: 2, y: 2, z: 4, core: 2. Of those that a mesh axis runs over, the one named last changes fastest.
Arguments:
- inputs: float32 [4, 1024, 2048], P('wsh', 'ctx'), may hold values from -6 to 6
- cotangent: float32 [4, 1024, 2048], P('wsh', 'ctx'), may hold values from -6 to 6
- block_order: int32 [4, 8], P('wsh'), may hold values from 0 to 7, each once within a row
- doc_cut: int32 [4], P('wsh'), may hold values from 256 to 768
- w_qkv: bfloat16 [2048, 6144], P(('ctx', 'wsh')), may hold values from -0.125 to 0.125
- b_qkv: bfloat16 [6144], P(('ctx', 'wsh')), may hold values from -3 to 3
- w_dense: bfloat16 [2048, 2048], P(('ctx', 'wsh')), may hold values from -0.75 to 0.75
- b_dense: bfloat16 [2048], P(('ctx', 'wsh')), may hold values from -4 to 4
- w_up: bfloat16 [2048, 8192], P(('ctx', 'wsh')), may hold values from -0.125 to 0.125
- b_up: bfloat16 [8192], P(('ctx', 'wsh')), may hold values from -3 to 3
- w_down: bfloat16 [8192, 2048], P(('ctx', 'wsh')), may hold values from -0.0625 to 0.0625
- b_down: bfloat16 [2048], P(('ctx', 'wsh')), may hold values from -4 to 4
- gain_attn: bfloat16 [2048], P(('ctx', 'wsh')), may hold values from 0.5 to 1.5
- shift_attn: bfloat16 [2048], P(('ctx', 'wsh')), may hold values from -3 to 3
- gain_mlp: bfloat16 [2048], P(('ctx', 'wsh')), may hold values from 0.099609375 to 1.8984375
- shift_mlp: bfloat16 [2048], P(('ctx', 'wsh')), may hold values from -3 to 3
Outputs:
- output: float32 [4, 1024, 2048], P('wsh', 'ctx')
- input_gradient: float32 [4, 1024, 2048], P('wsh', 'ctx')
- grad_w_qkv: float32 [2048, 6144], P(('ctx', 'wsh'))
- grad_b_qkv: float32 [6144], P(('ctx', 'wsh'))
- grad_w_dense: float32 [2048, 2048], P(('ctx', 'wsh'))
- grad_b_dense: float32 [2048], P(('ctx', 'wsh'))
- grad_w_up: float32 [2048, 8192], P(('ctx', 'wsh'))
- grad_b_up: float32 [8192], P(('ctx', 'wsh'))
- grad_w_down: float32 [8192, 2048], P(('ctx', 'wsh'))
- grad_b_down: float32 [2048], P(('ctx', 'wsh'))
- grad_gain_attn: float32 [2048], P(('ctx', 'wsh'))
- grad_shift_attn: float32 [2048], P(('ctx', 'wsh'))
- grad_gain_mlp: float32 [2048], P(('ctx', 'wsh'))
- grad_shift_mlp: float32 [2048], P(('ctx', 'wsh'))
Inputs may be any that keep to these rules, and one draw needn't show every extreme that they name: Each row is a permutation; ctx index i holds, in its first and second 128/2 rows, blocks block_order[s, i] and 15 - block_order[s, i] of the sequence.
All inputs are finite; a program needn't handle non-finite values.
Results may differ from a plain program's by a relative error of at most 0.019.
Values may be sent and summed in bfloat16 or wider, within the bound.
No kernel may reach another device: no remote copies, remote signals or barrier semaphores. Data moves between devices by JAX's collectives and lax.ppermute only.
A program may use at most 512 MiB of HBM per device.

v0:
```python
import jax
import jax.numpy as jnp
from jax import lax
from jax.sharding import PartitionSpec as P

HEADS = 8
HEAD_DIM = 256
ROT_DIM = 64


norm_eps = 1e-05
large_negative = -1e30


def normalize_layer(values, gain_vec, shift_vec):
    centre = values - jnp.mean(values, -1, keepdims=True)
    inv_std = lax.rsqrt(jnp.mean(centre * centre, -1, keepdims=True) + norm_eps)
    normed = centre * inv_std
    return (normed * gain_vec + shift_vec, normed, inv_std)


def norm_backward_pass(grad_out, normed, inv_std, gain_vec):
    scaled = grad_out * gain_vec
    return (
        scaled
        - jnp.mean(scaled, -1, keepdims=True)
        - normed * jnp.mean(scaled * normed, -1, keepdims=True)
    ) * inv_std


def rotate(values, places, direction):
    half_rot = ROT_DIM // 2
    frequency = jnp.power(10000.0, -2.0 * jnp.arange(half_rot).astype(jnp.float32) / ROT_DIM)
    angles = places.astype(jnp.float32)[:, None] * frequency[None, :]
    cos_part = jnp.cos(angles)[:, None, :]
    sine_part = jnp.sin(angles)[:, None, :]
    front_half = values[..., :half_rot]
    back_half = values[..., half_rot:ROT_DIM]
    return jnp.concatenate(
        [
            front_half * cos_part - direction * back_half * sine_part,
            back_half * cos_part + direction * front_half * sine_part,
            values[..., ROT_DIM:],
        ],
        -1,
    )


def gelu_parts(pre_act):
    normal_cdf = 0.5 * (1.0 + lax.erf(pre_act * 0.7071067811865476))
    density = jnp.exp(-0.5 * pre_act * pre_act) * 0.3989422804014327
    return (pre_act * normal_cdf, normal_cdf + pre_act * density)


def lookup_places(order_row, cut_value, offset, extent, tok_rows, ctx_count):
    row_index = offset + jnp.arange(extent, dtype=jnp.int32)
    device = row_index // tok_rows
    within = row_index % tok_rows
    half_dev = tok_rows // 2
    first_id = jnp.sum(
        jnp.where(
            device[:, None] == jnp.arange(ctx_count, dtype=jnp.int32)[None, :],
            order_row[None, :],
            0,
        ),
        1,
    )
    block_id = jnp.where(within < half_dev, first_id, 2 * ctx_count - 1 - first_id)
    places = block_id * half_dev + within % half_dev
    return (places, (places >= cut_value).astype(jnp.int32))


def allowed_mask(query_places, query_docs, key_places, key_docs):
    return (key_places[None, :] <= query_places[:, None]) & (
        key_docs[None, :] == query_docs[:, None]
    )


def body(
    inputs,
    cotangent,
    block_order,
    doc_cut,
    w_qkv,
    b_qkv,
    w_dense,
    b_dense,
    w_up,
    b_up,
    w_down,
    b_down,
    gain_attn,
    shift_attn,
    gain_mlp,
    shift_mlp,
):
    tok_rows = inputs.shape[1]
    width = inputs.shape[2]
    ctx_count = lax.axis_size("ctx")
    ctx_place = lax.axis_index("ctx")
    order_row = block_order[0]
    cut_value = doc_cut[0]
    local_input = inputs[0]
    local_grad = cotangent[0]
    gathered = (
        lax.all_gather(w_qkv, ("ctx", "wsh"), axis=0, tiled=True),
        lax.all_gather(b_qkv, ("ctx", "wsh"), axis=0, tiled=True),
        lax.all_gather(w_dense, ("ctx", "wsh"), axis=0, tiled=True),
        lax.all_gather(b_dense, ("ctx", "wsh"), axis=0, tiled=True),
        lax.all_gather(w_up, ("ctx", "wsh"), axis=0, tiled=True),
        lax.all_gather(b_up, ("ctx", "wsh"), axis=0, tiled=True),
        lax.all_gather(w_down, ("ctx", "wsh"), axis=0, tiled=True),
        lax.all_gather(b_down, ("ctx", "wsh"), axis=0, tiled=True),
        lax.all_gather(gain_attn, ("ctx", "wsh"), axis=0, tiled=True),
        lax.all_gather(shift_attn, ("ctx", "wsh"), axis=0, tiled=True),
        lax.all_gather(gain_mlp, ("ctx", "wsh"), axis=0, tiled=True),
        lax.all_gather(shift_mlp, ("ctx", "wsh"), axis=0, tiled=True),
    )
    (
        full_qkv,
        bias_qkv,
        full_dense,
        bias_dense,
        full_up,
        bias_up,
        full_down,
        bias_down,
        first_gain,
        first_shift,
        second_gain,
        second_shift,
    ) = gathered
    places, docs = lookup_places(
        order_row, cut_value, ctx_place * tok_rows, tok_rows, tok_rows, ctx_count
    )
    score_scale = HEAD_DIM ** (-0.5)
    first_normalized, first_centered_scaled, first_inverse_deviation = normalize_layer(
        local_input, first_gain, first_shift
    )
    second_normalized, second_centered_scaled, second_inverse_deviation = normalize_layer(
        local_input, second_gain, second_shift
    )
    first_in = first_normalized.astype(jnp.bfloat16)
    second_in = second_normalized.astype(jnp.bfloat16)
    projected = jnp.dot(first_in, full_qkv, preferred_element_type=jnp.float32) + bias_qkv
    queries = rotate(projected[:, :width].reshape(tok_rows, HEADS, HEAD_DIM), places, 1.0).astype(
        jnp.bfloat16
    )
    keys_local = rotate(
        projected[:, width : 2 * width].reshape(tok_rows, HEADS, HEAD_DIM), places, 1.0
    ).astype(jnp.bfloat16)
    values_local = projected[:, 2 * width :].reshape(tok_rows, HEADS, HEAD_DIM).astype(jnp.bfloat16)

    def piece_scores(arrived, offset):
        key_piece = arrived[0]
        key_places, key_docs = lookup_places(
            order_row, cut_value, offset, key_piece.shape[0], tok_rows, ctx_count
        )
        allowed = allowed_mask(places, docs, key_places, key_docs)[None]
        scores = (
            jnp.einsum("rhd,khd->hrk", queries, key_piece, preferred_element_type=jnp.float32)
            * score_scale
        )
        return (allowed, jnp.where(allowed, scores, large_negative))

    arrived = (
        lax.all_gather(keys_local, "ctx", axis=0, tiled=True),
        lax.all_gather(values_local, "ctx", axis=0, tiled=True),
    )
    running_max = jnp.full((HEADS, tok_rows), large_negative, jnp.float32)
    allowed, scores = piece_scores(arrived, jnp.int32(0))
    new_max = jnp.maximum(running_max, jnp.max(scores, -1))
    weights = jnp.where(allowed, jnp.exp(scores - new_max[..., None]), 0.0)
    running_sum = jnp.sum(weights, -1)
    weighted = jnp.einsum(
        "hrk,khd->rhd", weights.astype(jnp.bfloat16), arrived[1], preferred_element_type=jnp.float32
    )
    running_max, running_sum, weighted = (new_max, running_sum, weighted)
    log_total = running_max + jnp.log(running_sum)
    attended = (weighted / jnp.transpose(running_sum)[:, :, None]).astype(jnp.bfloat16)
    attn_flat = attended.reshape(tok_rows, width)
    attn_out = jnp.dot(attn_flat, full_dense, preferred_element_type=jnp.float32) + bias_dense
    pre_act = jnp.dot(second_in, full_up, preferred_element_type=jnp.float32) + bias_up
    activated, gelu_slope = gelu_parts(pre_act)
    hidden = activated.astype(jnp.bfloat16)
    output = (
        local_input
        + attn_out
        + (jnp.dot(hidden, full_down, preferred_element_type=jnp.float32) + bias_down)
    )
    back_qkv, back_dense, back_up, back_down = (full_qkv, full_dense, full_up, full_down)
    grad_rows = local_grad.astype(jnp.bfloat16)
    down_weight_gradient = jnp.einsum(
        "rf,rd->fd", hidden, grad_rows, preferred_element_type=jnp.float32
    )
    down_bias_gradient = jnp.sum(local_grad, 0)
    d_pre = jnp.dot(grad_rows, back_down.T, preferred_element_type=jnp.float32) * gelu_slope
    up_bias_gradient = jnp.sum(d_pre, 0)
    d_pre_b = d_pre.astype(jnp.bfloat16)
    up_weight_gradient = jnp.einsum(
        "rd,rf->df", second_in, d_pre_b, preferred_element_type=jnp.float32
    )
    second_norm_gradient = jnp.dot(d_pre_b, back_up.T, preferred_element_type=jnp.float32)
    second_gain_gradient = jnp.sum(second_norm_gradient * second_centered_scaled, 0)
    d_shift_two = jnp.sum(second_norm_gradient, 0)
    dense_weight_gradient = jnp.einsum(
        "re,rd->ed", attn_flat, grad_rows, preferred_element_type=jnp.float32
    )
    dense_bias_gradient = jnp.sum(local_grad, 0)
    d_attended = (
        jnp.dot(grad_rows, back_dense.T, preferred_element_type=jnp.float32)
        .astype(jnp.bfloat16)
        .reshape(tok_rows, HEADS, HEAD_DIM)
    )
    correction = jnp.einsum(
        "rhd,rhd->hr", d_attended.astype(jnp.float32), attended.astype(jnp.float32)
    )
    arrived = (
        lax.all_gather(keys_local, "ctx", axis=0, tiled=True),
        lax.all_gather(values_local, "ctx", axis=0, tiled=True),
    )
    key_piece, value_piece = arrived
    allowed, scores = piece_scores(arrived, jnp.int32(0))
    key_probs = jnp.where(allowed, jnp.exp(scores - log_total[..., None]), 0.0)
    value_term = jnp.einsum(
        "hrk,rhd->khd",
        key_probs.astype(jnp.bfloat16),
        d_attended,
        preferred_element_type=jnp.float32,
    )
    d_probs = jnp.einsum(
        "rhd,khd->hrk", d_attended, value_piece, preferred_element_type=jnp.float32
    )
    d_scores = (key_probs * (d_probs - correction[..., None]) * score_scale).astype(jnp.bfloat16)
    query_grad = jnp.einsum("hrk,khd->rhd", d_scores, key_piece, preferred_element_type=jnp.float32)
    key_term = jnp.einsum("hrk,rhd->khd", d_scores, queries, preferred_element_type=jnp.float32)
    key_grad = key_term
    value_grad = value_term
    query_grad, key_grad, value_grad = (query_grad, key_grad, value_grad)
    key_owned, value_owned = (
        lax.psum_scatter(
            key_grad.astype(jnp.bfloat16), "ctx", scatter_dimension=0, tiled=True
        ).astype(jnp.float32),
        lax.psum_scatter(
            value_grad.astype(jnp.bfloat16), "ctx", scatter_dimension=0, tiled=True
        ).astype(jnp.float32),
    )
    d_queries = rotate(query_grad, places, -1.0)
    d_keys = rotate(key_owned, places, -1.0)
    d_proj = jnp.concatenate(
        [
            d_queries.reshape(tok_rows, width),
            d_keys.reshape(tok_rows, width),
            value_owned.reshape(tok_rows, width),
        ],
        1,
    )
    projection_bias_gradient = jnp.sum(d_proj, 0)
    d_proj_b = d_proj.astype(jnp.bfloat16)
    projection_weight_gradient = jnp.einsum(
        "rd,re->de", first_in, d_proj_b, preferred_element_type=jnp.float32
    )
    first_norm_gradient = jnp.dot(d_proj_b, back_qkv.T, preferred_element_type=jnp.float32)
    first_gain_gradient = jnp.sum(first_norm_gradient * first_centered_scaled, 0)
    d_shift_one = jnp.sum(first_norm_gradient, 0)
    d_local = (
        local_grad
        + norm_backward_pass(
            first_norm_gradient, first_centered_scaled, first_inverse_deviation, first_gain
        )
        + norm_backward_pass(
            second_norm_gradient, second_centered_scaled, second_inverse_deviation, second_gain
        )
    )
    all_parts = (
        lax.psum_scatter(
            projection_weight_gradient, ("ctx", "wsh"), scatter_dimension=0, tiled=True
        ),
        lax.psum_scatter(projection_bias_gradient, ("ctx", "wsh"), scatter_dimension=0, tiled=True),
        lax.psum_scatter(dense_weight_gradient, ("ctx", "wsh"), scatter_dimension=0, tiled=True),
        lax.psum_scatter(dense_bias_gradient, ("ctx", "wsh"), scatter_dimension=0, tiled=True),
        lax.psum_scatter(up_weight_gradient, ("ctx", "wsh"), scatter_dimension=0, tiled=True),
        lax.psum_scatter(up_bias_gradient, ("ctx", "wsh"), scatter_dimension=0, tiled=True),
        lax.psum_scatter(down_weight_gradient, ("ctx", "wsh"), scatter_dimension=0, tiled=True),
        lax.psum_scatter(down_bias_gradient, ("ctx", "wsh"), scatter_dimension=0, tiled=True),
        lax.psum_scatter(first_gain_gradient, ("ctx", "wsh"), scatter_dimension=0, tiled=True),
        lax.psum_scatter(d_shift_one, ("ctx", "wsh"), scatter_dimension=0, tiled=True),
        lax.psum_scatter(second_gain_gradient, ("ctx", "wsh"), scatter_dimension=0, tiled=True),
        lax.psum_scatter(d_shift_two, ("ctx", "wsh"), scatter_dimension=0, tiled=True),
    )
    (
        grad_qkv,
        grad_bqkv,
        grad_dense,
        grad_bdense,
        grad_up,
        grad_bup,
        grad_down,
        grad_bdown,
        grad_gone,
        grad_sone,
        grad_gtwo,
        grad_stwo,
    ) = all_parts
    return (
        output.reshape(1, tok_rows, width),
        d_local.reshape(1, tok_rows, width),
        grad_qkv,
        grad_bqkv,
        grad_dense,
        grad_bdense,
        grad_up,
        grad_bup,
        grad_down,
        grad_bdown,
        grad_gone,
        grad_sone,
        grad_gtwo,
        grad_stwo,
    )


def solution(mesh):
    placed = (
        P("wsh", "ctx", None),
        P("wsh", "ctx", None),
        P("wsh", None),
        P("wsh"),
        P(("ctx", "wsh"), None),
        P(("ctx", "wsh")),
        P(("ctx", "wsh"), None),
        P(("ctx", "wsh")),
        P(("ctx", "wsh"), None),
        P(("ctx", "wsh")),
        P(("ctx", "wsh"), None),
        P(("ctx", "wsh")),
        P(("ctx", "wsh")),
        P(("ctx", "wsh")),
        P(("ctx", "wsh")),
        P(("ctx", "wsh")),
    )
    return jax.shard_map(
        body,
        mesh=mesh,
        in_specs=placed,
        out_specs=(
            P("wsh", "ctx", None),
            P("wsh", "ctx", None),
            P(("ctx", "wsh"), None),
            P(("ctx", "wsh")),
            P(("ctx", "wsh"), None),
            P(("ctx", "wsh")),
            P(("ctx", "wsh"), None),
            P(("ctx", "wsh")),
            P(("ctx", "wsh"), None),
            P(("ctx", "wsh")),
            P(("ctx", "wsh")),
            P(("ctx", "wsh")),
            P(("ctx", "wsh")),
            P(("ctx", "wsh")),
        ),
        check_vma=False,
    )
```

profile of v0, /device:TPU:0, one launch (start us, length us, event | category | flops | bytes accessed | tf_op | source)
XLA Modules:
  0.0 4640.3 jit_solution(13457321544980621494)
XLA Ops:
  14.7 43.8 all-reduce.15
  63.1 106.7 %all-gather.8.cloned.1.call-done = bf16[2048,6144]{1,0:T(8,128)(2,1)} async-done(((bf16[64,6144]{1,0:T(8,128)(2,1)}), bf16[2048,6144]{1,0:T(8,128)(2,1)}) %all-gather.8.cloned.1.call-update) | async-done | bytes 25165840 | tf_op jit(solution)/shard_map/all_gather | solution.py:106
  169.8 10.1 convolution_add_fusion.1
  186.9 61.3 %all-gather.14.cloned.1.call-done = bf16[2048,2048]{1,0:T(8,128)(2,1)} async-done(((bf16[64,2048]{1,0:T(8,128)(2,1)}), bf16[2048,2048]{1,0:T(8,128)(2,1)}) %all-gather.14.cloned.1.call-update) | async-done | bytes 8388624 | tf_op jit(solution)/shard_map/all_gather | solution.py:108
  248.2 6.3 fusion.78
  261.1 25.0 all-gather.12.cloned.1.call-done
  286.1 4.0 fusion.12
  293.3 32.5 all-gather.10.cloned.1.call-done
  325.8 6.2 multiply_reduce_fusion
  335.9 3.4 convert_bitcast_fusion
  340.4 5.6 convolution_convert_fusion
  346.0 6.7 copy.106
  354.9 67.5 %all-gather = bf16[32,1,256]{2,1,0:T(2,128)(2,1)S(1)} all-gather(bf16[1,1,256]{2,1,0:T(2,128)(2,1)S(1)} %reshape.349), channel_id=1, replica_groups=mesh['ctx'=8,'wsh'=4] {'ctx','wsh'}, dimensions={0}, use_global_device_ids=true | all-gather | bytes 16896 | tf_op jit(solution)/shard_map/all_gather | solution.py:111
  422.4 3.6 convolution_bitcast_fusion
  441.9 3.9 reduce-scatter.19.cloned.1.call-done
  451.2 15.6 fusion.62
  466.9 176.7 %all-gather.16.cloned.1.call-done = bf16[2048,8192]{1,0:T(8,128)(2,1)} async-done(((bf16[64,8192]{1,0:T(8,128)(2,1)}), bf16[2048,8192]{1,0:T(8,128)(2,1)}) %all-gather.16.cloned.1.call-update) | async-done | bytes 33554448 | tf_op jit(solution)/shard_map/all_gather | solution.py:110
  643.6 17.9 convolution_add_fusion
  661.5 178.1 %all-gather.18.cloned.1.call-done = bf16[8192,2048]{1,0:T(8,128)(2,1)} async-done(((bf16[256,2048]{1,0:T(8,128)(2,1)}), bf16[8192,2048]{1,0:T(8,128)(2,1)}) %all-gather.18.cloned.1.call-update) | async-done | bytes 33554448 | tf_op jit(solution)/shard_map/all_gather | solution.py:112
  839.5 18.8 fusion.76
  858.4 20.5 multiply_reduce_fusion.1
  879.0 8.1 fusion.38
  887.2 21.6 fusion.41
  908.8 24.9 fusion.31
  933.7 25.6 fusion.53
  960.1 5.8 fusion.9
  968.5 14.1 fusion.8
  982.5 18.6 all-reduce.18.cloned.1.call-done
  1009.6 359.7 %reduce-scatter.13.cloned.1.call-done = f32[64,2048]{1,0:T(8,128)} async-done(((f32[2048,2048]{1,0:T(8,128)}), f32[64,2048]{1,0:T(8,128)}) %reduce-scatter.13.cloned.1.call-update) | async-done | bytes 524304 | tf_op jit(solution)/shard_map/reduce_scatter | solution.py:280
  1369.3 437.5 %reduce-scatter.11.cloned.1.call-done = f32[64,6144]{1,0:T(8,128)} async-done(((f32[2048,6144]{1,0:T(8,128)}), f32[64,6144]{1,0:T(8,128)}) %reduce-scatter.11.cloned.1.call-update) | async-done | bytes 1572880 | tf_op jit(solution)/shard_map/reduce_scatter | solution.py:276
  1806.8 1412.6 %reduce-scatter.15.cloned.1.call-done = f32[64,8192]{1,0:T(8,128)} async-done(((f32[2048,8192]{1,0:T(8,128)}), f32[64,8192]{1,0:T(8,128)}) %reduce-scatter.15.cloned.1.call-update) | async-done | bytes 2097168 | tf_op jit(solution)/shard_map/reduce_scatter | solution.py:282
  3219.4 1413.7 %reduce-scatter.17.cloned.1.call-done = f32[256,2048]{1,0:T(8,128)} async-done(((f32[8192,2048]{1,0:T(8,128)}), f32[256,2048]{1,0:T(8,128)}) %reduce-scatter.17.cloned.1.call-update) | async-done | bytes 2097168 | tf_op jit(solution)/shard_map/reduce_scatter | solution.py:284
  (155 shorter events, 68.7 us)
Async XLA Ops:
  7.2 162.6 %copy-start = (f32[1,128,2048]{2,1,0:T(8,128)S(1)}, f32[1,128,2048]{2,1,0:T(8,128)}, u32[]{:S(2)}) copy-start(f32[1,128,2048]{2,1,0:T(8,128)} %param.16) | copy-start | bytes 3145732
  7.2 162.6 %all-gather.8.cloned.1.call-start = ((), (), s32[]{:S(2)}) async-start(), calls=%async_computation.6 | async-start | bytes 25952256 | tf_op jit(solution)/shard_map/all_gather | solution.py:106
  7.9 240.3 %all-gather.14.cloned.1.call-start = ((), (), s32[]{:S(2)}) async-start(), calls=%async_computation.9 | async-start | bytes 8650752 | tf_op jit(solution)/shard_map/all_gather | solution.py:108
  8.7 277.4 %all-gather.12.cloned.1.call-start = ((), (), s32[]{:S(2)}) async-start(), calls=%async_computation.8 | async-start | bytes 4718592 | tf_op jit(solution)/shard_map/all_gather | solution.py:167
  179.9 1.7 copy-start.7
  180.5 1.8 copy-start.9
  182.3 4.4 copy-start.19
  182.3 66.0 %copy-start.4 = (f32[1,128,2048]{2,1,0:T(8,128)S(1)}, f32[1,128,2048]{2,1,0:T(8,128)}, u32[]{:S(2)}) copy-start(f32[1,128,2048]{2,1,0:T(8,128)} %param.17) | copy-start | bytes 3145732
  184.0 141.8 %all-gather.10.cloned.1.call-start = ((), (), s32[]{:S(2)}) async-start(), calls=%async_computation.7 | async-start | bytes 4718592 | tf_op jit(solution)/shard_map/all_gather | solution.py:168
  186.4 242.0 %reduce-scatter.9.cloned.1.call-start = ((), (), s32[]{:S(2)}) async-start(), calls=%async_computation.12 | async-start | bytes 4718592 | tf_op jit(solution)/shard_map/reduce_scatter | solution.py:241
  290.0 2.0 copy-start.2
  325.8 6.2 copy-start.3
  325.8 6.2 copy-start.15
  325.8 6.4 copy-start.20
  334.6 1.3 copy-start.5
  339.3 1.0 copy-start.16
  339.3 106.5 %reduce-scatter.19.cloned.1.call-start = ((), (), s32[]{:S(2)}) async-start(), calls=%async_computation.17 | async-start | bytes 4718592
  352.6 2.2 copy-start.21
  352.7 290.9 %all-gather.16.cloned.1.call-start = ((), (), s32[]{:S(2)}) async-start(), calls=%async_computation.10 | async-start | bytes 34603008 | tf_op jit(solution)/shard_map/all_gather | solution.py:110
  353.4 486.1 %all-gather.18.cloned.1.call-start = ((), (), s32[]{:S(2)}) async-start(), calls=%async_computation.11 | async-start | bytes 34603008 | tf_op jit(solution)/shard_map/all_gather | solution.py:112
  354.2 647.0 %all-reduce.18.cloned.1.call-start = ((), (), s32[]{:S(2)}) async-start(), calls=%async_computation.18 | async-start | bytes 196608
  428.4 3.8 copy-start.12
  429.6 6.7 copy-start.10
  858.4 20.6 copy-start.11
  878.9 490.4 %reduce-scatter.13.cloned.1.call-start = ((), (), s32[]{:S(2)}) async-start(), calls=%async_computation.14 | async-start | bytes 17301504 | tf_op jit(solution)/shard_map/reduce_scatter | solution.py:280
  887.1 919.7 %reduce-scatter.11.cloned.1.call-start = ((), (), s32[]{:S(2)}) async-start(), calls=%async_computation.13 | async-start | bytes 51904512 | tf_op jit(solution)/shard_map/reduce_scatter | solution.py:276
  908.8 2310.6 %reduce-scatter.15.cloned.1.call-start = ((), (), s32[]{:S(2)}) async-start(), calls=%async_computation.15 | async-start | bytes 69206016 | tf_op jit(solution)/shard_map/reduce_scatter | solution.py:282
  933.7 3699.4 %reduce-scatter.17.cloned.1.call-start = ((), (), s32[]{:S(2)}) async-start(), calls=%async_computation.16 | async-start | bytes 69206016 | tf_op jit(solution)/shard_map/reduce_scatter | solution.py:284
  960.0 5.9 copy-start.13
  960.0 5.9 copy-start.14
  965.9 2.6 copy-start.1
  1001.9 3631.7 %copy-start.22 = (f32[64]{0:T(128)}, f32[64]{0:T(128)S(1)}, u32[]{:S(2)}) copy-start(f32[64]{0:T(128)S(1)} %dynamic-slice.1) | copy-start | bytes 772
  (4 other events, 3.3 us)
Sparse Core Ops, SparseCore 0:
  10.9 158.8 all-gather.7
  172.7 75.4 all-gather.13
  250.7 35.2 all-gather.11
  288.4 37.4 all-gather.9
  339.5 51.3 reduce-scatter.8
  394.5 51.3 reduce-scatter.18
  448.8 194.7 all-gather.15
  646.5 192.9 all-gather.17
  879.0 122.0 all-reduce.17
  1003.9 365.2 reduce-scatter.12
  1377.4 429.3 reduce-scatter.10
  1809.7 1409.6 reduce-scatter.14
  3222.4 1410.5 reduce-scatter.16
where the time goes:
time: 4650 us; the launch traced here: 4640 us
  waiting for transfers between devices  4230 us (91%)
  matrix products  215 us (5%)
  blocking collectives  111 us (2%)
  local copies, waits for them, and re-layouts  47.2 us (1%)
    reduce_scatter x1, waiting for transfers between devices, body(): lax.psum_scatter(down_weight_gradient, ('ctx', 'wsh'), scatter_dimension=...  1410 us
    reduce_scatter x1, waiting for transfers between devices, body(): lax.psum_scatter(up_weight_gradient, ('ctx', 'wsh'), scatter_dimension=0,...  1410 us
    reduce_scatter x1, waiting for transfers between devices, body(): lax.psum_scatter(projection_weight_gradient, ('ctx', 'wsh'), scatter_dime...  438 us
    reduce_scatter x1, waiting for transfers between devices, body(): lax.psum_scatter(dense_weight_gradient, ('ctx', 'wsh'), scatter_dimension...  360 us
    all_gather x1, waiting for transfers between devices, body(): lax.all_gather(w_down, ('ctx', 'wsh'), axis=0, tiled=True)  178 us
    all_gather x1, waiting for transfers between devices, body(): lax.all_gather(w_up, ('ctx', 'wsh'), axis=0, tiled=True)  177 us
    all_gather x1, waiting for transfers between devices, body(): lax.all_gather(w_qkv, ('ctx', 'wsh'), axis=0, tiled=True)  107 us
  transfers between devices with their start and end apart: 13, of which 12 were waited for; matrix products, arithmetic and copies ran while one was open for 5% of the time, Pallas kernels for 0%

commit v1 on v0

v1 whole, which is shorter than its diff:
```python
import jax
import jax.numpy as jnp
from jax import lax
from jax.experimental import pallas as pl
from jax.experimental.pallas import tpu as pltpu
from jax.sharding import PartitionSpec as P

HEADS = 8
HEAD_DIM = 256
ROT_DIM = 64
HALF = ROT_DIM // 2
NORM_EPS = 1e-05
LARGE_NEGATIVE = -1e30
SCALE = HEAD_DIM ** (-0.5)
f32 = jnp.float32
bf16 = jnp.bfloat16


def dot(a, b):
    return jnp.dot(a, b, preferred_element_type=f32)


def dot_t(a, b):
    return lax.dot_general(a, b, (((1,), (1,)), ((), ())), preferred_element_type=f32)


def t_dot(a, b):
    return lax.dot_general(a, b, (((0,), (0,)), ((), ())), preferred_element_type=f32)


def angles_of(places):
    frequency = jnp.power(10000.0, -2.0 * jnp.arange(HALF).astype(f32) / ROT_DIM)
    return places.astype(f32)[..., None] * frequency


def rotate(values, cos_part, sine_part):
    front = values[..., :HALF]
    back = values[..., HALF:ROT_DIM]
    return jnp.concatenate(
        [front * cos_part - back * sine_part, back * cos_part + front * sine_part, values[..., ROT_DIM:]], -1
    )


def gelu_parts(pre_act):
    normal_cdf = 0.5 * (1.0 + lax.erf(pre_act * 0.7071067811865476))
    density = jnp.exp(-0.5 * pre_act * pre_act) * 0.3989422804014327
    return (pre_act * normal_cdf, normal_cdf + pre_act * density)


def block_places(order, ctx_count, tok_rows):
    half = tok_rows // 2
    within = jnp.arange(tok_rows, dtype=jnp.int32)
    first = order[..., None]
    block = jnp.where(within < half, first, 2 * ctx_count - 1 - first)
    return block * half + within % half


def attention_kernel(x_ref, row_ref, key_ref, cos_ref, sin_ref, out_ref, dk_ref, dv_ref):
    length = x_ref.shape[0]
    hd = HEAD_DIM
    tile = min(256, length)
    lane = lax.broadcasted_iota(jnp.int32, (tile, 128), 1)

    def unrotate(value, rows):
        low = value[:, :128]
        other = jnp.where(lane < HALF, pltpu.roll(low, 128 - HALF, 1), pltpu.roll(low, HALF, 1))
        low = low * cos_ref[rows, :] + other * sin_ref[rows, :]
        return jnp.concatenate([low, value[:, 128:]], 1)

    keys = x_ref[:, hd : 2 * hd]
    values = x_ref[:, 2 * hd : 3 * hd]
    key_place = key_ref[0:1, :]
    for step in range(length // tile):
        rows = slice(step * tile, (step + 1) * tile)
        query = x_ref[rows, 0:hd]
        grad = x_ref[rows, 3 * hd : 4 * hd]
        place = row_ref[rows, 0:1]
        first = row_ref[rows, 1:2]
        allowed = (key_place <= place) & (key_place >= first)
        scores = jnp.where(allowed, dot_t(query, keys) * SCALE, LARGE_NEGATIVE)
        top = jnp.max(scores, 1, keepdims=True)
        weights = jnp.exp(scores - top)
        probs = weights * (1.0 / jnp.sum(weights, 1, keepdims=True))
        probs_b = probs.astype(bf16)
        attended = dot(probs_b, values).astype(bf16)
        out_ref[rows, 0:hd] = attended
        delta = jnp.sum(grad.astype(f32) * attended.astype(f32), 1, keepdims=True)
        d_probs = dot_t(grad, values)
        d_scores = (probs * (d_probs - delta) * SCALE).astype(bf16)
        out_ref[rows, hd : 2 * hd] = unrotate(dot(d_scores, keys), rows).astype(bf16)
        dk = t_dot(d_scores, query)
        dv = t_dot(probs_b, grad)
        if step == 0:
            dk_ref[...] = dk
            dv_ref[...] = dv
        else:
            dk_ref[...] += dk
            dv_ref[...] += dv
    for step in range(length // tile):
        rows = slice(step * tile, (step + 1) * tile)
        out_ref[rows, 2 * hd : 3 * hd] = unrotate(dk_ref[rows, :], rows).astype(bf16)
        out_ref[rows, 3 * hd : 4 * hd] = dv_ref[rows, :].astype(bf16)


def attention(packed, places, cut):
    length = packed.shape[0]
    angle = angles_of(places)
    cos, sin = jnp.cos(angle), jnp.sin(angle)
    rest = 128 - ROT_DIM
    cos_table = jnp.concatenate([cos, cos, jnp.ones((length, rest), f32)], 1)
    sin_table = jnp.concatenate([sin, -sin, jnp.zeros((length, rest), f32)], 1)
    first = jnp.where(places >= cut, cut, 0)
    row_info = jnp.stack([places, first], 1)
    key_info = places[None, :]
    return pl.pallas_call(
        attention_kernel,
        out_shape=jax.ShapeDtypeStruct((length, 4 * HEAD_DIM), bf16),
        in_specs=[pl.BlockSpec(memory_space=pltpu.VMEM)] * 5,
        out_specs=pl.BlockSpec(memory_space=pltpu.VMEM),
        scratch_shapes=[pltpu.VMEM((length, HEAD_DIM), f32), pltpu.VMEM((length, HEAD_DIM), f32)],
        compiler_params=pltpu.CompilerParams(vmem_limit_bytes=48 * 2**20),
        cost_estimate=pl.CostEstimate(
            flops=12 * length * length * HEAD_DIM,
            bytes_accessed=16 * length * HEAD_DIM,
            transcendentals=length * length,
        ),
    )(packed, row_info, key_info, cos_table, sin_table)


def body(
    inputs,
    cotangent,
    block_order,
    doc_cut,
    w_qkv,
    b_qkv,
    w_dense,
    b_dense,
    w_up,
    b_up,
    w_down,
    b_down,
    gain_attn,
    shift_attn,
    gain_mlp,
    shift_mlp,
):
    both = ("ctx", "wsh")
    C = lax.axis_size("ctx")
    W = lax.axis_size("wsh")
    c = lax.axis_index("ctx")
    z = lax.axis_index("wsh")
    T, D = inputs.shape[1:]
    DL = w_qkv.shape[0]
    FL = w_down.shape[0]
    E = D // W
    HL = HEADS // W
    PAIRS = W * HL
    R = C // PAIRS
    ROWS = W * T
    x = inputs[0]
    cot = cotangent[0]

    cut = doc_cut[0]
    ints = jnp.concatenate([block_order[0], (cut // 16)[None], (cut % 16)[None]]).astype(bf16)
    small = [b_qkv, b_dense, b_up, b_down, gain_attn, shift_attn, gain_mlp, shift_mlp, ints]
    sizes = [a.shape[0] for a in small]
    total = sum(sizes)
    width = -(-total // 128) * 128
    pack = jnp.concatenate(small + [jnp.zeros((width - total,), bf16)])
    pack = lax.all_gather(pack[None], both, axis=0, tiled=True)
    starts = [sum(sizes[:i]) for i in range(len(sizes))]
    pieces = [pack[:, s : s + n] for s, n in zip(starts, sizes)]
    bias_qkv, bias_dense, bias_up, bias_down, ga, sa, gm, sm = [p.reshape(-1) for p in pieces[:-1]]
    info = pieces[-1][:W].astype(f32).astype(jnp.int32)
    orders = info[:, :C]
    cuts = info[:, C] * 16 + info[:, C + 1]
    bias_qkv = lax.dynamic_slice_in_dim(bias_qkv.reshape(3, W, E), z, 1, 1).reshape(3 * E)
    bias_up = lax.dynamic_slice_in_dim(bias_up.reshape(C, W, FL), z, 1, 1).reshape(C * FL)

    part_qkv = w_qkv.reshape(DL, 3, W, E).transpose(2, 0, 1, 3).reshape(W, DL, 3 * E)
    part_up = w_up.reshape(DL, C, W, FL).transpose(2, 0, 1, 3).reshape(W, DL, C * FL)
    turned = lax.all_to_all(jnp.concatenate([part_qkv, part_up], 2), "wsh", 0, 0, tiled=True)
    turned = turned.reshape(W * DL, 3 * E + C * FL)
    moves = [(i, (i % C) * W + i // C) for i in range(C * W)]
    back_moves = [(j, i) for i, j in moves]
    full_dense = lax.all_gather(lax.ppermute(w_dense, both, moves), "ctx", axis=0, tiled=True)
    full_down = lax.all_gather(w_down, "ctx", axis=0, tiled=True)
    full_qkv = lax.all_gather(turned[:, : 3 * E], "ctx", axis=0, tiled=True)
    full_up = lax.all_gather(turned[:, 3 * E :], "ctx", axis=0, tiled=True)

    centre = x - jnp.mean(x, -1, keepdims=True)
    inv_std = lax.rsqrt(jnp.mean(centre * centre, -1, keepdims=True) + NORM_EPS)
    normed = centre * inv_std
    xh = lax.all_gather(normed.astype(bf16), "wsh", axis=0, tiled=True)
    g = lax.all_gather(cot.astype(bf16), "wsh", axis=0, tiled=True)
    xh32 = xh.astype(f32)
    h_attn = (xh32 * ga + sa).astype(bf16)
    h_mlp = (xh32 * gm + sm).astype(bf16)

    own_angle = angles_of(block_places(lax.dynamic_index_in_dim(orders, c, 1, False), C, T))[:, :, None, None, :]
    proj = (dot(h_attn, full_qkv) + bias_qkv).reshape(W, T, 3, HL, HEAD_DIM)
    q_k = rotate(proj[:, :, :2], jnp.cos(own_angle), jnp.sin(own_angle)).astype(bf16)
    d_att = dot_t(g, full_dense).astype(bf16).reshape(W, T, 1, HL, HEAD_DIM)
    send = jnp.concatenate([q_k, proj[:, :, 2:].astype(bf16), d_att], 2)
    send = send.transpose(0, 3, 1, 2, 4).reshape(PAIRS, T, 4 * HEAD_DIM)
    if R > 1:
        send = jnp.repeat(send, R, 0)
    packed = lax.all_to_all(send, "ctx", 0, 0, tiled=True).reshape(C * T, 4 * HEAD_DIM)
    seq = c // R // HL
    seq_order = lax.dynamic_index_in_dim(orders, seq, 0, False)
    seq_cut = lax.dynamic_index_in_dim(cuts, seq, 0, False)
    result = attention(packed, block_places(seq_order, C, T).reshape(-1), seq_cut)
    result = lax.all_to_all(result.reshape(C, T, 4 * HEAD_DIM), "ctx", 0, 0, tiled=True)
    if R > 1:
        result = result.reshape(PAIRS, R, T, 4 * HEAD_DIM)[:, 0]
    result = result.reshape(W, HL, T, 4, HEAD_DIM).transpose(3, 0, 2, 1, 4).reshape(4, ROWS, E)
    attended = result[0]
    d_proj = result[1:].transpose(1, 0, 2).reshape(ROWS, 3 * E)

    pre = dot(h_mlp, full_up) + bias_up
    activated, slope = gelu_parts(pre)
    hidden = activated.astype(bf16)
    d_pre = dot_t(g, full_down) * slope
    d_pre_b = d_pre.astype(bf16)
    gw_down = t_dot(hidden, g).astype(bf16)
    gw_up = t_dot(h_mlp, d_pre_b).astype(bf16)
    d_h_mlp = dot_t(d_pre_b, full_up)

    def scatter(value, axis):
        return lax.psum_scatter(value, axis, scatter_dimension=0, tiled=True)

    out_part = dot(hidden, full_down) + dot(attended, full_dense)
    out_sum = scatter(out_part.astype(bf16), "wsh").astype(f32)
    output = x + out_sum + bias_dense + bias_down

    gw_dense = t_dot(attended, g).astype(bf16)
    gw_qkv = t_dot(h_attn, d_proj).astype(bf16)
    d_h_attn = dot_t(d_proj, full_qkv)

    e = scatter((d_h_attn * ga + d_h_mlp * gm).astype(bf16), "wsh").astype(f32)
    input_gradient = (
        cot + (e - jnp.mean(e, -1, keepdims=True) - normed * jnp.mean(e * normed, -1, keepdims=True)) * inv_std
    )

    grad_down = scatter(gw_down, "ctx").astype(f32)
    grad_dense = lax.ppermute(scatter(gw_dense, "ctx"), both, back_moves).astype(f32)
    own_up = scatter(gw_up, "ctx").reshape(W, DL, C * FL)
    own_qkv = scatter(gw_qkv, "ctx").reshape(W, DL, 3 * E)
    turned = lax.all_to_all(jnp.concatenate([own_qkv, own_up], 2), "wsh", 0, 0, tiled=True).astype(f32)
    grad_qkv = turned[:, :, : 3 * E].reshape(W, DL, 3, E).transpose(1, 2, 0, 3).reshape(DL, 3 * D)
    grad_up = turned[:, :, 3 * E :].reshape(W, DL, C, FL).transpose(1, 2, 0, 3).reshape(DL, C * W * FL)

    gb_qkv = jnp.zeros((3, W, E), f32)
    gb_qkv = lax.dynamic_update_slice_in_dim(gb_qkv, jnp.sum(d_proj.astype(f32), 0).reshape(3, 1, E), z, 1)
    gb_up = jnp.zeros((C, W, FL), f32)
    gb_up = lax.dynamic_update_slice_in_dim(gb_up, jnp.sum(d_pre, 0).reshape(C, 1, FL), z, 1)
    vectors = [
        gb_qkv,
        jnp.sum(cot, 0),
        gb_up,
        jnp.sum(d_h_attn * xh32, 0),
        jnp.sum(d_h_attn, 0),
        jnp.sum(d_h_mlp * xh32, 0),
        jnp.sum(d_h_mlp, 0),
    ]
    vectors = [v.reshape(C * W, -1) for v in vectors]
    lengths = [v.shape[1] for v in vectors]
    summed = jnp.sum(lax.all_to_all(jnp.concatenate(vectors, 1), both, 0, 0, tiled=True), 0)
    marks = [sum(lengths[:i]) for i in range(len(lengths))]
    gb_qkv, gb_dense, gb_up, g_ga, g_sa, g_gm, g_sm = [summed[m : m + n] for m, n in zip(marks, lengths)]
    return (
        output[None],
        input_gradient[None],
        grad_qkv,
        gb_qkv,
        grad_dense,
        gb_dense,
        grad_up,
        gb_up,
        grad_down,
        gb_dense,
        g_ga,
        g_sa,
        g_gm,
        g_sm,
    )


def solution(mesh):
    tokens = P("wsh", "ctx", None)
    matrix = P(("ctx", "wsh"), None)
    vector = P(("ctx", "wsh"))
    pairs = (matrix, vector) * 4
    return jax.shard_map(
        body,
        mesh=mesh,
        in_specs=(tokens, tokens, P("wsh", None), P("wsh")) + pairs + (vector,) * 4,
        out_specs=(tokens, tokens) + pairs + (vector,) * 4,
        check_vma=False,
    )
```

time: 4650 us -> 753 us (0.16)
  waiting for transfers between devices: 4230 us -> 350 us
  matrix products: 215 us -> 87.4 us
  blocking collectives: 111 us -> 188 us
    reduce_scatter x5 -> x6, waiting for transfers between devices: 3620 us -> 272 us  [scatter(): return lax.psum_scatter(value, axis, scatter_dimension=0, tiled=True)]
    all_gather x6, waiting for transfers between devices: 580 us -> 34.3 us  [the longest x1 31.3 us: body(): full_qkv = lax.all_gather(turned[:, :3 * E], 'ctx', axis=0, tiled=True)]
    dot_general x18 -> x12, matrix products: 215 us -> 87.4 us  [the longest x4 30.1 us: dot_t(): lax.dot_general(a, b, (((1,), (1,)), ((), ())), preferred_element_type=f32)]
    all_to_all x0 -> x2, blocking collectives: none -> 119 us  [the longest x1 83.1 us: body(): lax.all_to_all(jnp.concatenate([part_qkv, part_up], 2), 'wsh', 0, 0, tile...]
  transfers between devices with their start and end apart: 13 -> 17, of which waited for: 12 -> 8; matrix products, arithmetic and copies ran while one was open for 5% -> 19% of each run, Pallas kernels for 0% -> 1%
where the time goes in v1:
time: 753 us; the launch traced here: 748 us
  waiting for transfers between devices  350 us (46%)
  blocking collectives  188 us (25%)
  matrix products  87.4 us (12%)
  local copies, waits for them, and re-layouts  53.5 us (7%)
  other arithmetic  29.7 us (4%)
  starting transfers between devices  17.1 us (2%)
  between operations  16.2 us (2%)
    reduce_scatter x6, waiting for transfers between devices, scatter(): return lax.psum_scatter(value, axis, scatter_dimension=0, tiled=True)  272 us
    all_to_all x1, blocking collectives, body(): lax.all_to_all(jnp.concatenate([part_qkv, part_up], 2), 'wsh', 0, 0, tile...  83.1 us
    all_gather x1, blocking collectives, body(): pack = lax.all_gather(pack[None], both, axis=0, tiled=True)  68.7 us
    all_to_all x1, waiting for transfers between devices, body(): lax.all_to_all(send, 'ctx', 0, 0, tiled=True).reshape(C * T, 4 * HEAD_DIM)  43.7 us
    all_to_all x1, blocking collectives, body(): lax.all_to_all(result.reshape(C, T, 4 * HEAD_DIM), 'ctx', 0, 0, tiled=True)  35.9 us
    all_gather x1, waiting for transfers between devices, body(): full_qkv = lax.all_gather(turned[:, :3 * E], 'ctx', axis=0, tiled=True)  31.3 us
    dot_general x4, matrix products, dot_t(): lax.dot_general(a, b, (((1,), (1,)), ((), ())), preferred_element_type=f32)  30.1 us
    dot_general x4, matrix products, t_dot(): lax.dot_general(a, b, (((0,), (0,)), ((), ())), preferred_element_type=f32)  28.9 us
  transfers between devices with their start and end apart: 17, of which 8 were waited for; matrix products, arithmetic and copies ran while one was open for 19% of the time, Pallas kernels for 1%

profile of v1, /device:TPU:0, one launch (start us, length us, event | category | flops | bytes accessed | tf_op | source)
XLA Modules:
  0.0 748.5 jit_solution(11367586458918299484)
XLA Ops:
  19.4 83.1 %all_to_all.29 = bf16[4,64,3584]{2,1,0:T(8,128)(2,1)S(1)} all-to-all(bf16[4,64,3584]{2,1,0:T(8,128)(2,1)S(1)} %pad_maximum_fusion), channel_id=1, replica_groups=mesh['ctx'=8,'wsh'=4] {'wsh'}, dimensions={0} | all-to-all | bytes 3670016 | tf_op jit(solution)/shard_map/all_to_all | solution.py:183
  106.2 68.7 %all-gather.1 = bf16[32,1,896]{2,1,0:T(2,128)(2,1)S(1)} all-gather(bf16[1,1,896]{2,1,0:T(2,128)(2,1)S(1)} %reshape.477), channel_id=2, replica_groups=mesh['ctx'=8,'wsh'=4] {'ctx','wsh'}, dimensions={0}, use_global_device_ids=true | all-gather | bytes 59136 | tf_op jit(solution)/shard_map/all_gather | solution.py:171
  177.6 3.5 convolution_convert_fusion.4
  182.1 31.3 %all-gather.15.cloned.1.call-done = bf16[2048,1536]{1,0:T(8,128)(2,1)} async-done(((bf16[256,1536]{1,0:T(8,128)(2,1)}), bf16[2048,1536]{1,0:T(8,128)(2,1)}) %all-gather.15.cloned.1.call-update) | async-done | bytes 6291472 | tf_op jit(solution)/shard_map/all_gather | solution.py:189
  213.4 8.5 %convolution_add_fusion = f32[512,1536]{1,0:T(8,128)} fusion(bf16[2048,1536]{1,0:T(8,128)(2,1)} %all-gather.15.cloned.1.call-done, bf16[512,2048]{1,0:T(8,128)(2,1)} %all-gather.9.cloned.1.call-done, f32[2048]{0:T(1024)S(1)} %reshape.472, f32[2048]{0:T(1024)S(1)} %reshape.471, f32[1536]{0:T(1024)S(1)} %reshape.473), kind=kOutput, calls=%fused_computation.23 | convolution fusion | flops 3226206208 | bytes 11556864 | tf_op jit(solution)/shard_map/dot_general | solution.py:20
  221.9 3.9 reshape.446
  230.5 4.8 maximum_bitcast_fusion
  238.9 4.0 all-to-all-start.1
  247.8 43.7 %all-to-all-done.1 = bf16[8,128,1024]{2,1,0:T(8,128)(2,1)S(1)} async-done(((bf16[8,128,1024]{2,1,0:T(8,128)(2,1)}), bf16[8,128,1024]{2,1,0:T(8,128)(2,1)S(1)}, u32[]{:S(2)}, u32[]{:S(2)}) %all-to-all-start.1) | async-done | bytes 2097184 | tf_op jit(solution)/shard_map/all_to_all | solution.py:209
  292.6 6.5 shard_map.263
  300.4 3.2 copy.82
  303.6 35.9 %all_to_all.30 = bf16[8,128,1024]{1,2,0:T(8,128)(2,1)S(1)} all-to-all(bf16[8,128,1024]{1,2,0:T(8,128)(2,1)S(1)} %copy.82), channel_id=1, replica_groups=mesh['ctx'=8,'wsh'=4] {'ctx'}, dimensions={0} | all-to-all | bytes 4194304 | tf_op jit(solution)/shard_map/all_to_all | solution.py:214
  344.1 7.7 %convolution_convert_fusion.2 = bf16[2048,1536]{1,0:T(8,128)(2,1)} fusion(bf16[512,1536]{0,1:T(8,128)(2,1)S(1)} %bitcast.122, bf16[512,2048]{1,0:T(8,128)(2,1)} %all-gather.9.cloned.1.call-done, f32[2048]{0:T(1024)S(1)} %copy-done.12, f32[2048]{0:T(1024)S(1)} %reshape.471), kind=kOutput, calls=%fused_computation.2 | convolution fusion | flops 3228565504 | bytes 9977856 | tf_op jit(solution)/shard_map/dot_general | solution.py:28
  352.1 9.6 %multiply_convert_fusion = (bf16[512,2048]{1,0:T(8,128)(2,1)}, f32[512,2048]{1,0:T(8,128)}) fusion(f32[2048]{0:T(1024)S(1)} %bitcast.133, bf16[2048,2048]{1,0:T(8,128)(2,1)} %all-gather.11.cloned.1.call-done, bf16[512,2048]{1,0:T(8,128)(2,1)} %all-gather.9.cloned.1.call-done, f32[2048]{0:T(1024)S(1)} %reshape.469, f32[2048]{0:T(1024)S(1)} %reshape.468), kind=kOutput, calls=%fused_computation.21 | convolution fusion | flops 4305453056 | bytes 16801792 | tf_op jit(solution)/shard_map/dot_general | solution.py:20
  364.7 9.6 %fusion.36 = (f32[2048]{0:T(1024)S(1)}, bf16[512,2048]{1,0:T(8,128)(2,1)S(1)}) fusion(f32[512,2048]{1,0:T(8,128)} %get-tuple-element.52, f32[2048]{0:T(1024)S(1)} %bitcast.134, bf16[512,2048]{1,0:T(8,128)(2,1)} %all-gather.17.cloned.1.call-done, bf16[2048,2048]{1,0:T(8,128)(2,1)} %all-gather.13.cloned.1.call-done), kind=kOutput, calls=%fused_computation.97 | convolution fusion | flops 4307548160 | bytes 16793600 | tf_op jit(solution)/shard_map/dot_general | solution.py:24
  375.6 6.8 convolution_convert_fusion.1
  384.2 4.2 convolution_convert_fusion.3
  388.5 6.4 fusion.38
  394.9 10.5 %fusion.31 = (f32[2048]{0:T(1024)S(1)}, f32[2048]{0:T(1024)S(1)}, bf16[512,2048]{1,0:T(8,128)(2,1)}, f32[2048]{0:T(1024)S(1)}, f32[2048]{0:T(1024)S(1)}) fusion(bf16[512,2048]{1,0:T(8,128)(2,1)S(1)} %copy-done.31, f32[2048]{0:T(1024)S(1)} %reshape.468, f32[512,2048]{1,0:T(8,128)S(1)} %fusion.38, f32[2048]{0:T(1024)S(1)} %reshape.471, ...), kind=kOutput, calls=%fused_computation.93 | convolution fusion | flops 4306493440 | bytes 18923520 | tf_op jit(solution)/shard_map/dot_general | solution.py:24
  405.5 7.7 %fusion.37 = f32[512,2048]{1,0:T(8,128)S(1)} fusion(bf16[512,2048]{1,0:T(8,128)(2,1)} %get-tuple-element.51, bf16[2048,2048]{1,0:T(8,128)(2,1)} %all-gather.13.cloned.1.call-done), kind=kOutput, calls=%fused_computation.98 | convolution fusion | flops 4294967296 | bytes 14680064 | tf_op jit(solution)/shard_map/dot_general | solution.py:20
  416.0 10.2 %convolution_convert_fusion = bf16[2048,2048]{1,0:T(8,128)(2,1)} fusion(bf16[512,2048]{1,0:T(8,128)(2,1)} %get-tuple-element.51, bf16[512,2048]{1,0:T(8,128)(2,1)} %all-gather.17.cloned.1.call-done), kind=kOutput, calls=%fused_computation | convolution fusion | flops 4299161600 | bytes 12582912 | tf_op jit(solution)/shard_map/dot_general | solution.py:28
  427.9 4.6 all-to-all-start.4
  432.5 72.5 %reduce-scatter.13.cloned.1.call-done = bf16[256,2048]{1,0:T(8,128)(2,1)} async-done(((bf16[2048,2048]{1,0:T(8,128)(2,1)}), bf16[256,2048]{1,0:T(8,128)(2,1)}) %reduce-scatter.13.cloned.1.call-update) | async-done | bytes 1048592 | tf_op jit(solution)/shard_map/reduce_scatter | solution.py:231
  505.0 3.0 pad_maximum_fusion.1
  508.0 4.6 all-to-all-start.3
  512.6 36.9 %reduce-scatter.15.cloned.1.call-done = bf16[64,2048]{1,0:T(8,128)(2,1)} async-done(((bf16[512,2048]{1,0:T(8,128)(2,1)}), bf16[64,2048]{1,0:T(8,128)(2,1)}) %reduce-scatter.15.cloned.1.call-update) | async-done | bytes 262160 | tf_op jit(solution)/shard_map/reduce_scatter | solution.py:231
  554.1 45.5 %reduce-scatter.9.cloned.1.call-done = bf16[128,2048]{1,0:T(8,128)(2,1)} async-done(((bf16[512,2048]{1,0:T(8,128)(2,1)}), bf16[128,2048]{1,0:T(8,128)(2,1)}) %reduce-scatter.9.cloned.1.call-update) | async-done | bytes 524304 | tf_op jit(solution)/shard_map/reduce_scatter | solution.py:231
  601.0 45.8 %reduce-scatter.7.cloned.1.call-done = bf16[128,2048]{1,0:T(8,128)(2,1)} async-done(((bf16[512,2048]{1,0:T(8,128)(2,1)}), bf16[128,2048]{1,0:T(8,128)(2,1)}) %reduce-scatter.7.cloned.1.call-update) | async-done | bytes 524304 | tf_op jit(solution)/shard_map/reduce_scatter | solution.py:231
  646.8 3.5 fusion.19
  650.3 70.9 %reduce-scatter.17.cloned.1.call-done = bf16[256,2048]{1,0:T(8,128)(2,1)} async-done(((bf16[2048,2048]{1,0:T(8,128)(2,1)}), bf16[256,2048]{1,0:T(8,128)(2,1)}) %reduce-scatter.17.cloned.1.call-update) | async-done | bytes 1048592 | tf_op jit(solution)/shard_map/reduce_scatter | solution.py:231
  727.8 3.3 reshape.467
  737.4 3.2 reshape.456
  (206 shorter events, 68.7 us)
Async XLA Ops:
  7.2 6.1 copy-start.2
  7.2 7.4 copy-start.9
  7.2 170.4 %all-gather.17.cloned.1.call-start = ((), (), s32[]{:S(2)}) async-start(), calls=%async_computation.15 | async-start | bytes 2621440 | tf_op jit(solution)/shard_map/all_gather | solution.py:196
  9.5 168.1 %all-gather.19.cloned.1.call-start = ((), (), s32[]{:S(2)}) async-start(), calls=%async_computation.16 | async-start | bytes 2359296 | tf_op jit(solution)/shard_map/all_gather | solution.py:187
  9.5 1.6 collective-permute-start
  11.9 170.2 %all-gather.9.cloned.1.call-start = ((), (), s32[]{:S(2)}) async-start(), calls=%async_computation.11 | async-start | bytes 2621440 | tf_op jit(solution)/shard_map/all_gather | solution.py:195
  14.6 198.8 %all-gather.15.cloned.1.call-start = ((), (), s32[]{:S(2)}) async-start(), calls=%async_computation.14 | async-start | bytes 7077888 | tf_op jit(solution)/shard_map/all_gather | solution.py:189
  103.5 248.6 %all-gather.11.cloned.1.call-start = ((), (), s32[]{:S(2)}) async-start(), calls=%async_computation.12 | async-start | bytes 9437184 | tf_op jit(solution)/shard_map/all_gather | solution.py:190
  104.7 260.0 %all-gather.13.cloned.1.call-start = ((), (), s32[]{:S(2)}) async-start(), calls=%async_computation.13 | async-start | bytes 9437184 | tf_op jit(solution)/shard_map/all_gather | solution.py:188
  175.2 38.2 %copy-start.11 = (f32[2048]{0:T(1024)}, f32[2048]{0:T(1024)S(1)}, u32[]{:S(2)}) copy-start(f32[2048]{0:T(1024)S(1)} %reshape.472) | copy-start | bytes 24580
  175.5 5.6 copy-start.17
  236.2 7.6 %copy-start.18 = (pred[128]{0:T(512)(128)(4,1)S(1)}, pred[128]{0:T(512)(128)(4,1)}, u32[]{:S(2)}) copy-start(pred[128]{0:T(512)(128)(4,1)} %copy-done.17) | copy-start | bytes 388
  236.2 7.6 %copy-start.20 = (s32[128]{0:T(128)S(1)}, s32[128]{0:T(128)}, u32[]{:S(2)}) copy-start(s32[128]{0:T(128)} %copy-done.19) | copy-start | bytes 1540
  236.2 9.4 %copy-start.16 = (f32[32]{0:T(128)S(1)}, f32[32]{0:T(128)}, u32[]{:S(2)}) copy-start(f32[32]{0:T(128)} %copy-done.15) | copy-start | bytes 388
  238.9 52.6 %all-to-all-start.1 = ((bf16[8,128,1024]{2,1,0:T(8,128)(2,1)}), bf16[8,128,1024]{2,1,0:T(8,128)(2,1)S(1)}, u32[]{:S(2)}, u32[]{:S(2)}) async-start(bf16[8,128,1024]{2,1,0:T(8,128)(2,1)} %reshape.448), calls=%async_computation.1 | async-start | bytes 4194304 | tf_op jit(solution)/shard_map/all_to_all | solution.py:209
  242.9 189.6 %reduce-scatter.11.cloned.1.call-start = ((), (), s32[]{:S(2)}) async-start(), calls=%async_computation.19 | async-start | bytes 7077888 | tf_op jit(solution)/shard_map/reduce_scatter | solution.py:231
  344.1 7.7 %copy-start.7 = (bf16[512,3,512]{0,2,1:T(8,128)(2,1)}, bf16[512,3,512]{0,2,1:T(8,128)(2,1)S(1)}, u32[]{:S(2)}) copy-start(bf16[512,3,512]{0,2,1:T(8,128)(2,1)S(1)} %copy.85) | copy-start | bytes 4718596
  351.8 153.2 %reduce-scatter.13.cloned.1.call-start = ((), (), s32[]{:S(2)}) async-start(), calls=%async_computation.20 | async-start | bytes 9437184 | tf_op jit(solution)/shard_map/reduce_scatter | solution.py:231
  364.7 10.9 %copy-start.30 = (bf16[512,2048]{1,0:T(8,128)(2,1)S(1)}, bf16[512,2048]{1,0:T(8,128)(2,1)}, u32[]{:S(2)}) copy-start(bf16[512,2048]{1,0:T(8,128)(2,1)} %all-gather.9.cloned.1.call-done) | copy-start | bytes 6291460
  382.5 167.1 %reduce-scatter.15.cloned.1.call-start = ((), (), s32[]{:S(2)}) async-start(), calls=%async_computation.21 | async-start | bytes 2359296 | tf_op jit(solution)/shard_map/reduce_scatter | solution.py:231
  388.4 211.2 %reduce-scatter.9.cloned.1.call-start = ((), (), s32[]{:S(2)}) async-start(), calls=%async_computation.18 | async-start | bytes 2621440 | tf_op jit(solution)/shard_map/reduce_scatter | solution.py:231
  388.4 6.5 copy-start.31
  388.4 6.5 copy-start.34
  405.5 241.3 %reduce-scatter.7.cloned.1.call-start = ((), (), s32[]{:S(2)}) async-start(), calls=%async_computation.17 | async-start | bytes 2621440 | tf_op jit(solution)/shard_map/reduce_scatter | solution.py:231
  405.5 7.7 %copy-start.6 = (bf16[512,2048]{1,0:T(8,128)(2,1)S(1)}, bf16[512,2048]{1,0:T(8,128)(2,1)}, u32[]{:S(2)}) copy-start(bf16[512,2048]{1,0:T(8,128)(2,1)} %all-gather.19.cloned.1.call-done) | copy-start | bytes 6291460
  415.9 305.2 %reduce-scatter.17.cloned.1.call-start = ((), (), s32[]{:S(2)}) async-start(), calls=%async_computation.22 | async-start | bytes 9437184 | tf_op jit(solution)/shard_map/reduce_scatter | solution.py:231
  427.9 80.1 %all-to-all-start.4 = ((f32[32,1,768]{2,1,0:T(1,128)}), f32[32,1,768]{2,1,0:T(1,128)S(1)}, u32[]{:S(2)}, u32[]{:S(2)}) async-start(f32[32,1,768]{2,1,0:T(1,128)} %all_to_all.22), calls=%async_computation.8 | async-start | bytes 196608 | tf_op jit(solution)/shard_map/all_to_all | solution.py:269
  505.0 94.6 %copy-start.3 = (f32[1,128,2048]{2,1,0:T(8,128)S(1)}, f32[1,128,2048]{2,1,0:T(8,128)}, u32[]{:S(2)}) copy-start(f32[1,128,2048]{2,1,0:T(8,128)} %param.16) | copy-start | bytes 3145732
  505.0 94.6 %copy-start.14 = (f32[128]{0:T(128)S(1)}, f32[128]{0:T(128)}, u32[]{:S(2)}) copy-start(f32[128]{0:T(128)} %copy-done.13) | copy-start | bytes 1540
  508.0 216.0 %all-to-all-start.3 = ((bf16[4,64,3584]{2,1,0:T(8,128)(2,1)}), bf16[4,64,3584]{2,1,0:T(8,128)(2,1)S(1)}, u32[]{:S(2)}, u32[]{:S(2)}) async-start(bf16[4,64,3584]{2,1,0:T(8,128)(2,1)} %pad_maximum_fusion.1), calls=%async_computation.7 | async-start | bytes 3670016 | tf_op jit(solution)/shard_map/all_to_all | solution.py:250
  549.5 3.8 collective-permute-start.1
  553.3 187.4 %copy-start.29 = (f32[64]{0:T(128)}, f32[64]{0:T(128)S(1)}, u32[]{:S(2)}) copy-start(f32[64]{0:T(128)S(1)} %get-tuple-element.82) | copy-start | bytes 772
  (20 other events, 58.0 us)
Sparse Core Ops, SparseCore 0:
  10.2 79.0 all-gather.16
  91.8 25.5 all-gather.18
  119.5 47.1 all-gather.8
  169.0 44.3 all-gather.14
  215.7 76.4 all-gather.10
  293.9 70.6 all-gather.12
  368.0 61.7 reduce-scatter.10
  433.7 71.2 reduce-scatter.12
  508.3 41.1 reduce-scatter.14
  552.3 47.2 reduce-scatter.8
  601.9 44.8 reduce-scatter.6
  650.5 70.6 reduce-scatter.16

commit v2 on v1

v2 whole, which is shorter than its diff:
```python
import jax
import jax.numpy as jnp
from jax import lax
from jax.experimental import pallas as pl
from jax.experimental.pallas import tpu as pltpu
from jax.sharding import Mesh
from jax.sharding import PartitionSpec as P

HEADS = 8
HEAD_DIM = 256
ROT_DIM = 64
HALF = ROT_DIM // 2
NORM_EPS = 1e-05
LARGE_NEGATIVE = -1e30
SCALE = HEAD_DIM ** (-0.5)
f32 = jnp.float32
bf16 = jnp.bfloat16


def dot(a, b):
    return jnp.dot(a, b, preferred_element_type=f32)


def dot_t(a, b):
    return lax.dot_general(a, b, (((1,), (1,)), ((), ())), preferred_element_type=f32)


def t_dot(a, b):
    return lax.dot_general(a, b, (((0,), (0,)), ((), ())), preferred_element_type=f32)


def angles_of(places):
    frequency = jnp.power(10000.0, -2.0 * jnp.arange(HALF).astype(f32) / ROT_DIM)
    return places.astype(f32)[..., None] * frequency


def gelu_parts(pre_act):
    normal_cdf = 0.5 * (1.0 + lax.erf(pre_act * 0.7071067811865476))
    density = jnp.exp(-0.5 * pre_act * pre_act) * 0.3989422804014327
    return (pre_act * normal_cdf, normal_cdf + pre_act * density)


def block_places(order, ctx_count, tok_rows):
    half = tok_rows // 2
    within = jnp.arange(tok_rows, dtype=jnp.int32)
    first = order[..., None]
    block = jnp.where(within < half, first, 2 * ctx_count - 1 - first)
    return block * half + within % half


VMEM_LIMIT = 56 * 2**20


def rotary_tables(places, direction):
    angle = angles_of(places)
    cos, sin = jnp.cos(angle), jnp.sin(angle) * direction
    rest = 128 - ROT_DIM
    ones = jnp.ones((places.shape[0], rest), f32)
    return jnp.concatenate([cos, cos, ones], 1), jnp.concatenate([-sin, sin, 0.0 * ones], 1)


def turn(value, cos, sin):
    low = value[:, :128]
    lane = lax.broadcasted_iota(jnp.int32, low.shape, 1)
    other = jnp.where(lane < HALF, pltpu.roll(low, 128 - HALF, 1), pltpu.roll(low, HALF, 1))
    return jnp.concatenate([low * cos + other * sin, value[:, 128:]], 1)


class Columns:
    def __init__(self, array, unit, j):
        self.array, self.unit, self.j = array, unit, j
        self.shape = array.shape[:-1] + (unit,)
        self.dtype = array.dtype
        self.size = array.size // array.shape[-1] * unit


def columns(array, unit, first, last):
    return [Columns(array, unit, j) for j in range(first, last)]


def call(kernel, outs, operands, flops, scratch=(), scalar=None):
    moved = sum(o.size * o.dtype.itemsize for o in list(operands) + list(outs))
    in_specs, arrays = [], []
    if scalar is not None:
        in_specs.append(pl.BlockSpec(memory_space=pltpu.SMEM))
        arrays.append(scalar.reshape(1).astype(jnp.int32))
    for operand in operands:
        if isinstance(operand, Columns):
            lead = (0,) * (len(operand.shape) - 1)
            in_specs.append(pl.BlockSpec(operand.shape, lambda i, lead=lead, j=operand.j: lead + (j,)))
            arrays.append(operand.array)
        else:
            zero = (0,) * len(operand.shape)
            in_specs.append(pl.BlockSpec(operand.shape, lambda i, zero=zero: zero))
            arrays.append(operand)
    out_specs = [pl.BlockSpec(o.shape, lambda i, zero=(0,) * len(o.shape): zero) for o in outs]
    return pl.pallas_call(
        kernel,
        grid=(1,),
        out_shape=outs,
        in_specs=in_specs,
        out_specs=out_specs,
        scratch_shapes=list(scratch),
        compiler_params=pltpu.CompilerParams(vmem_limit_bytes=VMEM_LIMIT),
        cost_estimate=pl.CostEstimate(flops=flops, bytes_accessed=moved, transcendentals=0),
    )(*arrays)


def kept_block(p, count, core):
    half = count // 2
    return 2 * (p % half) + (core if p < half else 1 - core)


def kept_difference(p, count):
    half = count // 2
    return 2 * (p % half) + p // half


def at(index, size):
    return pl.ds(pl.multiple_of(index * size, size), size)


def shaped(shape, dtype):
    return jax.ShapeDtypeStruct(shape, dtype)


def attention_kernel(x_ref, row_ref, key_ref, cos_ref, sin_ref, out_ref, dk_ref, dv_ref):
    length = x_ref.shape[0]
    hd = HEAD_DIM
    tile = min(256, length)
    keys = x_ref[:, hd : 2 * hd]
    values = x_ref[:, 2 * hd : 3 * hd]
    key_place = key_ref[0:1, :]
    for step in range(length // tile):
        rows = slice(step * tile, (step + 1) * tile)
        query = x_ref[rows, 0:hd]
        grad = x_ref[rows, 3 * hd : 4 * hd]
        place = row_ref[rows, 0:1]
        first = row_ref[rows, 1:2]
        allowed = (key_place <= place) & (key_place >= first)
        scores = jnp.where(allowed, dot_t(query, keys) * SCALE, LARGE_NEGATIVE)
        top = jnp.max(scores, 1, keepdims=True)
        weights = jnp.exp(scores - top)
        probs = weights * (1.0 / jnp.sum(weights, 1, keepdims=True))
        probs_b = probs.astype(bf16)
        attended = dot(probs_b, values).astype(bf16)
        out_ref[rows, 0:hd] = attended
        delta = jnp.sum(grad.astype(f32) * attended.astype(f32), 1, keepdims=True)
        d_probs = dot_t(grad, values)
        d_scores = (probs * (d_probs - delta) * SCALE).astype(bf16)
        d_query = dot(d_scores, keys)
        out_ref[rows, hd : 2 * hd] = turn(d_query, cos_ref[rows, :], sin_ref[rows, :]).astype(bf16)
        dk = t_dot(d_scores, query)
        dv = t_dot(probs_b, grad)
        if step == 0:
            dk_ref[...] = dk
            dv_ref[...] = dv
        else:
            dk_ref[...] += dk
            dv_ref[...] += dv
    for step in range(length // tile):
        rows = slice(step * tile, (step + 1) * tile)
        out_ref[rows, 2 * hd : 3 * hd] = turn(dk_ref[rows, :], cos_ref[rows, :], sin_ref[rows, :]).astype(bf16)
        out_ref[rows, 3 * hd : 4 * hd] = dv_ref[rows, :].astype(bf16)


def attention(packed, places, cut):
    length = packed.shape[0]
    cos_table, sin_table = rotary_tables(places, -1.0)
    first = jnp.where(places >= cut, cut, 0)
    row_info = jnp.stack([places, first], 1)
    operands = (packed, row_info, places[None, :], cos_table, sin_table)
    scratch = [pltpu.VMEM((length, HEAD_DIM), f32), pltpu.VMEM((length, HEAD_DIM), f32)]
    outs = [shaped((length, 4 * HEAD_DIM), bf16)]
    return call(attention_kernel, outs, operands, 12 * length * length * HEAD_DIM, scratch)[0]


def project(acts, gain, shift_by, held, bias, cos, sin, part, tokens, index):
    rows, width = acts.shape[0], acts.shape[1] // 2
    count, unit = held.shape[0], held.shape[2] // 8
    seqs = rows // tokens
    hd = HEAD_DIM
    heads = unit // hd
    pieces = width // unit
    size = part // pieces

    def kernel(*refs):
        index_ref, acts_ref, gain_ref, shift_ref, bias_ref, cos_ref, sin_ref = refs[:7]
        w_refs, dense_in_ref = refs[7:10], refs[10]
        send_ref, h_ref, dense_ref = refs[11:]
        core = index_ref[0] & 1
        for p in range(count):
            for j in range(pieces):
                block = dense_in_ref[p, j * size : (j + 1) * size, :]
                dense_ref[p * size : (p + 1) * size, j * unit : (j + 1) * unit] = block
            cols = at(kept_block(p, count, core), part)
            h = acts_ref[:, cols].astype(f32) * gain_ref[0:1, cols] + shift_ref[0:1, cols]
            h_ref[:, p * part : (p + 1) * part] = h.astype(bf16)
        for head in range(heads):
            for piece in range(3):
                start = (head * 3 + piece) * hd
                total = jnp.broadcast_to(bias_ref[0:1, start : start + hd], (rows, hd))
                w_ref, start = w_refs[start // unit], start % unit
                for p in range(count):
                    block = w_ref[kept_block(p, count, core), :part, start : start + hd]
                    total = total + dot(h_ref[:, p * part : (p + 1) * part], block)
                if piece < 2:
                    total = turn(total, cos_ref[...], sin_ref[...])
                send_ref[:, head, :, piece * hd : (piece + 1) * hd] = total.astype(bf16).reshape(seqs, tokens, hd)
            d_att = dot_t(acts_ref[:, width:], dense_ref[head * hd : (head + 1) * hd, :])
            send_ref[:, head, :, 3 * hd :] = d_att.astype(bf16).reshape(seqs, tokens, hd)

    outs = [
        shaped((seqs, heads, tokens, 4 * hd), bf16),
        shaped((rows, width), bf16),
        shaped((unit, width), bf16),
    ]
    operands = [acts, gain[None], shift_by[None], bias[None], cos, sin]
    operands += columns(held, unit, 0, 4)
    return call(kernel, outs, operands, 8 * rows * width * unit, scalar=index)


def feed_forward(acts, gain, shift_by, held, bias, down_blocks, part, index):
    rows, width = acts.shape[0], acts.shape[1] // 2
    count, unit = held.shape[0], held.shape[2] // 8
    size = down_blocks[0].shape[0]
    hidden_n = 4 * unit
    tile = 256

    def kernel(*refs):
        index_ref, acts_ref, gain_ref, shift_ref, bias_ref = refs[:5]
        up_refs = refs[5:9]
        down_refs = refs[9 : 9 + count]
        h_ref, hidden_ref, d_pre_ref, out_ref, sum_ref, down_ref = refs[9 + count :]
        core = index_ref[0] & 1
        for p in range(count):
            down_ref[at(index_ref[0] ^ kept_difference(p, count), size), :] = down_refs[p][...]
            cols = at(kept_block(p, count, core), part)
            h = acts_ref[:, cols].astype(f32) * gain_ref[0:1, cols] + shift_ref[0:1, cols]
            h_ref[:, p * part : (p + 1) * part] = h.astype(bf16)
        for step in range(hidden_n // tile):
            cols = slice(step * tile, (step + 1) * tile)
            up_ref, start = up_refs[step * tile // unit], step * tile % unit
            pre = jnp.broadcast_to(bias_ref[0:1, cols], (rows, tile))
            for p in range(count):
                block = up_ref[kept_block(p, count, core), :part, start : start + tile]
                pre = pre + dot(h_ref[:, p * part : (p + 1) * part], block)
            activated, slope = gelu_parts(pre)
            hidden_ref[:, cols] = activated.astype(bf16)
            d_pre = dot_t(acts_ref[:, width:], down_ref[cols, :]) * slope
            sum_ref[0:1, cols] = jnp.sum(d_pre, 0, keepdims=True)
            d_pre_ref[:, cols] = d_pre.astype(bf16)
        for step in range(width // 256):
            cols = slice(step * 256, (step + 1) * 256)
            out_ref[:, cols] = dot(hidden_ref[...], down_ref[:, cols])

    outs = [
        shaped((rows, width), bf16),
        shaped((rows, hidden_n), bf16),
        shaped((rows, hidden_n), bf16),
        shaped((rows, width), f32),
        shaped((1, hidden_n), f32),
    ]
    operands = [acts, gain[None], shift_by[None], bias[None]] + columns(held, unit, 4, 8) + list(down_blocks)
    scratch = [pltpu.VMEM((hidden_n, width), bf16)]
    return call(kernel, outs, operands, 6 * rows * width * hidden_n, scratch, scalar=index)


def input_terms(d_out, held, first, acts, gain, part, e_before=None):
    rows, width = acts.shape[0], acts.shape[1] // 2
    count, unit = held.shape[0], held.shape[2] // 8
    units = d_out.shape[1] // unit

    def kernel(*refs):
        d_out_ref, acts_ref, gain_ref = refs[:3]
        w_refs = refs[3 : 3 + units]
        e_ref, sum_ref = refs[-2:]
        for p in range(count):
            cols = slice(p * part, (p + 1) * part)
            d_h = dot_t(d_out_ref[:, :unit], w_refs[0][p, :part, :])
            for j in range(1, units):
                d_h = d_h + dot_t(d_out_ref[:, j * unit : (j + 1) * unit], w_refs[j][p, :part, :])
            sum_ref[0:1, cols] = jnp.sum(d_h * acts_ref[:, cols].astype(f32), 0, keepdims=True)
            sum_ref[1:2, cols] = jnp.sum(d_h, 0, keepdims=True)
            e = d_h * gain_ref[0:1, cols]
            if e_before is not None:
                e = e + refs[3 + units][:, cols]
            e_ref[:, cols] = e.astype(e_ref.dtype)

    outs = [shaped((rows, width), f32 if e_before is None else bf16), shaped((2, width), f32)]
    operands = [d_out, acts, gain[None]] + columns(held, unit, first, first + units)
    if e_before is not None:
        operands.append(e_before)
    return call(kernel, outs, operands, 2 * rows * width * d_out.shape[1])


def split_columns(w_qkv, w_up, wsh, ctx):
    rows = w_qkv.shape[0]
    width = w_qkv.shape[1] // 3
    hd = HEAD_DIM
    heads = HEADS // wsh
    fl = w_up.shape[1] // (ctx * wsh)

    def kernel(qkv_ref, up_ref, out_ref):
        for z in range(wsh):
            for head in range(heads):
                for piece in range(3):
                    start = piece * width + (z * heads + head) * hd
                    to = (head * 3 + piece) * hd
                    out_ref[z, :, to : to + hd] = qkv_ref[:, start : start + hd]
            out_ref[z, :, 3 * heads * hd :] = jnp.concatenate(
                [up_ref[:, (c * wsh + z) * fl : (c * wsh + z + 1) * fl] for c in range(ctx)], 1
            )

    outs = [shaped((wsh, rows, 3 * heads * hd + ctx * fl), bf16)]
    return call(kernel, outs, (w_qkv, w_up), 0)[0]


def join_qkv(parts, columns):
    wsh, rows, _ = parts.shape
    hd = HEAD_DIM
    heads = HEADS // wsh

    def kernel(in_ref, out_ref):
        for z in range(wsh):
            for head in range(heads):
                for piece in range(3):
                    to = piece * HEADS * hd + (z * heads + head) * hd
                    start = (head * 3 + piece) * hd
                    out_ref[:, to : to + hd] = in_ref[z, :, start : start + hd].astype(f32)

    return call(kernel, [shaped((rows, wsh * columns), f32)], (parts,), 0)[0]


def join_up(parts, first, ctx):
    wsh, rows, columns = parts.shape
    fl = (columns - first) // ctx

    def kernel(in_ref, out_ref):
        for c in range(ctx):
            start = first + c * fl
            out_ref[:, c * wsh * fl : (c + 1) * wsh * fl] = jnp.concatenate(
                [in_ref[z, :, start : start + fl].astype(f32) for z in range(wsh)], 1
            )

    return call(kernel, [shaped((rows, wsh * (columns - first)), f32)], (parts,), 0)[0]


def unpack(result):
    seqs, heads, tokens, _ = result.shape
    hd = HEAD_DIM
    rows = seqs * tokens

    def kernel(in_ref, att_ref, proj_ref, sum_ref):
        for head in range(heads):
            value = in_ref[:, head].reshape(rows, 4 * hd)
            att_ref[:, head * hd : (head + 1) * hd] = value[:, :hd]
            proj_ref[:, head * 3 * hd : (head + 1) * 3 * hd] = value[:, hd:]
            sum_ref[0:1, head * 3 * hd : (head + 1) * 3 * hd] = jnp.sum(value[:, hd:].astype(f32), 0, keepdims=True)

    outs = [
        shaped((rows, heads * hd), bf16),
        shaped((rows, heads * 3 * hd), bf16),
        shaped((1, heads * 3 * hd), f32),
    ]
    return call(kernel, outs, (result,), 0)


CTX = ("chip", "core")


def after(value, *others):
    return lax.optimization_barrier((value,) + others)[0]


def hop(value):
    return lax.ppermute(value, "core", [(0, 1), (1, 0)])


def exchange(value, axis):
    return lax.all_to_all(value, axis, 0, 0, tiled=True)


def chip_hop(value, k):
    n = lax.axis_size("chip")
    return lax.ppermute(value, "chip", [(i, i ^ k) for i in range(n)])


def shift(value, step):
    n = lax.axis_size("wsh")
    return lax.ppermute(value, "wsh", [(i, (i + step) % n) for i in range(n)])


def chip_blocks(block):
    return [block] + [chip_hop(block, k) for k in range(1, lax.axis_size("chip"))]


def with_other_core(own):
    return list(own) + [hop(value) for value in own]


def sum_arrived(value):
    return jnp.sum(value.astype(f32), 0).astype(bf16)


def over_cores(value):
    core = lax.axis_index("core")
    away = hop(lax.dynamic_index_in_dim(value, 1 - core, 1, False))
    return (lax.dynamic_index_in_dim(value, core, 1, False).astype(f32) + away.astype(f32)).astype(bf16)


def hop_terms(terms):
    return [chip_hop(term, k) for k, term in enumerate(terms) if k]


def sum_terms(own, arrived):
    total = own.astype(f32)
    for term in arrived:
        total = total + term.astype(f32)
    return total.astype(bf16)


def body(
    inputs,
    cotangent,
    block_order,
    doc_cut,
    w_qkv,
    b_qkv,
    w_dense,
    b_dense,
    w_up,
    b_up,
    w_down,
    b_down,
    gain_attn,
    shift_attn,
    gain_mlp,
    shift_mlp,
):
    both = CTX + ("wsh",)
    C = lax.axis_size(CTX)
    W = lax.axis_size("wsh")
    core = lax.axis_index("core")
    c = lax.axis_index(CTX)
    z = lax.axis_index("wsh")
    T, D = inputs.shape[1:]
    DL = w_qkv.shape[0]
    FL = w_down.shape[0]
    E = D // W
    HL = HEADS // W
    PAIRS = W * HL
    R = C // PAIRS
    PART = D // C
    x = inputs[0]
    cot = cotangent[0]

    moves = [(i, (i % C) * W + i // C) for i in range(C * W)]
    back_moves = [(j, i) for i, j in moves]
    own_down = chip_blocks(w_down)
    moved_dense = lax.ppermute(w_dense, both, moves)

    centre = x - jnp.mean(x, -1, keepdims=True)
    inv_std = lax.rsqrt(jnp.mean(centre * centre, -1, keepdims=True) + NORM_EPS)
    normed = centre * inv_std
    acts = jnp.concatenate([normed.astype(bf16), cot.astype(bf16)], 1)
    cut = doc_cut[0]
    ints = jnp.concatenate([block_order[0], (cut // 16)[None], (cut % 16)[None]]).astype(bf16)
    small = [b_qkv, b_dense, b_up, b_down, gain_attn, shift_attn, gain_mlp, shift_mlp, ints]
    sizes = [a.shape[0] for a in small]
    starts = [sum(sizes[:i]) for i in range(len(sizes))]
    rider = jnp.concatenate(small + [jnp.zeros((3 * E - sum(sizes),), bf16)])
    turned = exchange(split_columns(w_qkv, w_up, W, C), "wsh")
    rider = jnp.broadcast_to(rider, (16, 3 * E))
    riders = jnp.broadcast_to(rider[:1], (16, 3 * E))
    for k in range(1, W):
        riders = lax.dynamic_update_slice_in_dim(riders, shift(rider, k)[:1], (z - k) % W, 0)
    riders = lax.dynamic_update_slice_in_dim(riders, rider[:1], z, 0)
    turned, acts, riders, moved_dense, *own_down = lax.optimization_barrier((turned, acts, riders, moved_dense, *own_down))
    dense_part = moved_dense.reshape(DL, W, E).transpose(1, 0, 2).reshape(W * DL, E)
    turned = turned.reshape(W * DL, 7 * E)
    held = jnp.concatenate([turned[:, : 3 * E], dense_part, turned[:, 3 * E :]], 1)
    held = jnp.concatenate([held, jnp.pad(riders, ((0, 0), (0, 5 * E)))], 0)
    held = lax.all_gather(held[None], CTX, axis=0, tiled=True)
    acts_all = jnp.zeros((W, T, 2 * D), bf16)
    acts_all = lax.dynamic_update_slice_in_dim(acts_all, acts[None], z, 0)
    for k in range(1, W):
        acts_all = lax.dynamic_update_slice_in_dim(acts_all, shift(acts, k)[None], (z - k) % W, 0)
    acts = acts_all.reshape(W * T, 2 * D)
    g = acts[:, D:]
    blocks_down = with_other_core(own_down)
    held, acts, *blocks_down = lax.optimization_barrier((held, acts, *blocks_down))
    pack = held[:, W * DL : W * DL + W, : 3 * E]
    pieces = [pack[:, :, s : s + n].astype(f32) for s, n in zip(starts, sizes)]
    bias_qkv, bias_dense, bias_up, bias_down, ga, sa, gm, sm = [p.reshape(-1) for p in pieces[:8]]
    info = pieces[-1][0].astype(jnp.int32)
    orders = info[:, :C]
    cuts = info[:, C] * 16 + info[:, C + 1]
    bias_qkv = lax.dynamic_index_in_dim(bias_qkv.reshape(3, W, HL, HEAD_DIM), z, 1, False).transpose(1, 0, 2).reshape(3 * E)
    bias_up = lax.dynamic_index_in_dim(pieces[2], z, 1, False).reshape(C * FL)

    own_places = block_places(lax.dynamic_index_in_dim(orders, c, 1, False), C, T).reshape(-1)
    own_cos, own_sin = rotary_tables(own_places, 1.0)
    send, h_attn, full_dense = project(acts, ga, sa, held, bias_qkv, own_cos, own_sin, PART, T, c)
    send = send.reshape(PAIRS, T, 4 * HEAD_DIM)
    if R > 1:
        send = jnp.repeat(send, R, 0)
    packed = exchange(send, CTX).reshape(C * T, 4 * HEAD_DIM)

    h_mlp, hidden, d_pre, out_mlp, sum_pre = feed_forward(
        after(acts, send), gm, sm, held, bias_up, blocks_down, PART, c
    )
    seq = c // R // HL
    seq_order = lax.dynamic_index_in_dim(orders, seq, 0, False)
    seq_cut = lax.dynamic_index_in_dim(cuts, seq, 0, False)
    result = attention(after(packed, d_pre), block_places(seq_order, C, T).reshape(-1), seq_cut)

    h_late = after(h_mlp, result)
    result = exchange(result.reshape(C, T, 4 * HEAD_DIM), CTX)
    away_up = hop(t_dot(h_late[:, D // 2 :], d_pre).astype(bf16))
    gw_down = t_dot(after(hidden, away_up), g).astype(bf16)
    kept_up = (t_dot(h_late[:, : D // 2], d_pre) + away_up.astype(f32)).astype(bf16)
    kept_down = over_cores(gw_down.reshape(C // 2, 2, FL, D))
    result = after(result, kept_up, kept_down)
    arrived_up = exchange(after(kept_up, result).reshape(C // 2, PART, C * FL), "chip")
    if R > 1:
        result = result.reshape(PAIRS, R, T, 4 * HEAD_DIM)[:, 0]
    attended, d_proj, sum_proj = unpack(result.reshape(W, HL, T, 4 * HEAD_DIM))
    away_qkv = t_dot(h_attn[:, D // 2 :], d_proj).astype(bf16)
    out_part = (out_mlp + dot(after(attended, away_qkv), full_dense)).astype(bf16)
    away_here = hop(away_qkv)
    out_sum = lax.psum_scatter(out_part.reshape(W * T, D), "wsh", scatter_dimension=0, tiled=True)
    gw_dense = t_dot(attended, g).astype(bf16)
    kept_qkv = (t_dot(after(h_attn, out_part)[:, : D // 2], d_proj) + away_here.astype(f32)).astype(bf16)
    e_mlp, sums_mlp = input_terms(after(d_pre, kept_qkv), held, 4, acts, gm, PART)
    e_mlp, arrived_up = lax.optimization_barrier((e_mlp, arrived_up))
    arrived_qkv = exchange(after(kept_qkv, arrived_up).reshape(C // 2, PART, 3 * E), "chip")
    e_part, sums_attn = input_terms(d_proj, held, 0, acts, ga, PART, e_mlp)
    e_part, out_sum = lax.optimization_barrier((e_part, out_sum))
    e_sum = lax.psum_scatter(e_part, "wsh", scatter_dimension=0, tiled=True)

    kept_dense = over_cores(after(gw_dense, e_part).reshape(C // 2, 2, DL, D))
    own_up = sum_arrived(after(arrived_up, e_part))
    arrived_qkv = after(arrived_qkv, own_up, kept_dense)
    own_grads = jnp.concatenate([sum_arrived(arrived_qkv), own_up], 1)
    back = exchange(own_grads.reshape(W, DL, 7 * E), "wsh")
    kept_down = after(kept_down, arrived_qkv)
    terms = [lax.dynamic_index_in_dim(kept_down, lax.axis_index("chip") ^ k, 0, False) for k in range(C // 2)]
    grad_down = terms[0].astype(f32)
    for term in hop_terms(terms):
        grad_down = grad_down + term.astype(f32)
    terms = [lax.dynamic_index_in_dim(kept_dense, lax.axis_index("chip") ^ k, 0, False) for k in range(C // 2)]
    grad_dense = lax.ppermute(sum_terms(terms[0], hop_terms(terms)), both, back_moves).astype(f32)

    output = x + out_sum.astype(f32) + (bias_dense + bias_down)
    e = e_sum.astype(f32)
    input_gradient = (
        cot + (e - jnp.mean(e, -1, keepdims=True) - normed * jnp.mean(e * normed, -1, keepdims=True)) * inv_std
    )
    grad_qkv = join_qkv(after(back, grad_down), 3 * E)
    grad_up = join_up(back, 3 * E, C)

    sum_proj = sum_proj.reshape(HL, 3, HEAD_DIM).transpose(1, 0, 2).reshape(3, 1, E)
    gb_qkv = lax.dynamic_update_slice_in_dim(jnp.zeros((3, W, E), f32), sum_proj, z, 1).reshape(C * W, -1)
    gb_up = lax.dynamic_update_slice_in_dim(jnp.zeros((C, W, FL), f32), sum_pre.reshape(C, 1, FL), z, 1)
    gb_up = gb_up.reshape(C * W, FL)
    by_width = jnp.concatenate([sums_attn, sums_mlp, jnp.sum(cot, 0, keepdims=True)], 0)
    by_width = by_width.reshape(5, C * W, DL).transpose(1, 0, 2).reshape(C * W, 5 * DL)
    vectors = jnp.concatenate([gb_up, gb_qkv, by_width], 1)
    summed = jnp.sum(exchange(after(vectors, own_grads), both), 0)
    n_up, n_qkv = gb_up.shape[1], gb_qkv.shape[1]
    gb_up, gb_qkv = summed[:n_up], summed[n_up : n_up + n_qkv]
    g_ga, g_sa, g_gm, g_sm, gb_dense = [
        summed[n_up + n_qkv + i * DL : n_up + n_qkv + (i + 1) * DL] for i in range(5)
    ]
    return (
        output[None],
        input_gradient[None],
        grad_qkv,
        gb_qkv,
        grad_dense,
        gb_dense,
        grad_up,
        gb_up,
        grad_down,
        gb_dense,
        g_ga,
        g_sa,
        g_gm,
        g_sm,
    )


def solution(mesh):
    ctx, wsh = mesh.shape["ctx"], mesh.shape["wsh"]
    split = Mesh(mesh.devices.reshape(ctx // 2, 2, wsh), CTX + ("wsh",))
    tokens = P("wsh", CTX, None)
    matrix = P(CTX + ("wsh",), None)
    vector = P(CTX + ("wsh",))
    pairs = (matrix, vector) * 4
    return jax.shard_map(
        body,
        mesh=split,
        in_specs=(tokens, tokens, P("wsh", None), P("wsh")) + pairs + (vector,) * 4,
        out_specs=(tokens, tokens) + pairs + (vector,) * 4,
        check_vma=False,
    )
```

time: 753 us -> 531 us (0.71)
  blocking collectives: 188 us -> 14.3 us
  waiting for transfers between devices: 350 us -> 232 us
  Pallas kernels: 6.5 us -> 80.4 us
  matrix products: 87.4 us -> 35.8 us
  starting transfers between devices: 17.1 us -> 63.5 us
  local copies, waits for them, and re-layouts: 53.5 us -> 35.5 us
  other arithmetic: 29.7 us -> 44.4 us
    reduce_scatter x6 -> x2, waiting for transfers between devices: 272 us -> 0.02 us  [the longest x1 0.02 us: body(): lax.psum_scatter(out_part.reshape(W * T, D), 'wsh', scatter_dimension=0,...]
    ppermute x2 -> x25, waiting for transfers between devices: 0.01 us -> 153 us  [the longest x6 90.9 us: shift(): return lax.ppermute(value, 'wsh', [(i, (i + step) % n) for i in range(n)])]
    all_to_all x2 -> x1, blocking collectives: 119 us -> 14.3 us  [exchange(): return lax.all_to_all(value, axis, 0, 0, tiled=True)]
    pallas_call x1 -> x9, Pallas kernels: 6.5 us -> 80.4 us  [call(): pl.pallas_call(kernel, grid=(1,), out_shape=outs, in_specs=in_specs, out_...]
    all_gather x1 -> x0, blocking collectives: 68.7 us -> none  [body(): pack = lax.all_gather(pack[None], both, axis=0, tiled=True)]
    ppermute x2 -> x25, starting transfers between devices: 3.43 us -> 36.6 us  [the longest x6 18.8 us: shift(): return lax.ppermute(value, 'wsh', [(i, (i + step) % n) for i in range(n)])]
    dot_general x4 -> x0, matrix products: 30.1 us -> none  [dot_t(): lax.dot_general(a, b, (((1,), (1,)), ((), ())), preferred_element_type=f32)]
    reshape x22 -> x6, local copies, waits for them, and re-layouts: 27.8 us -> 0.38 us  [the longest x1 0.18 us: body(): moved_dense.reshape(DL, W, E).transpose(1, 0, 2).reshape(W * DL, E)]
  transfers between devices with their start and end apart: 17 -> 34, of which waited for: 8 -> 16; matrix products, arithmetic and copies ran while one was open for 19% -> 14% of each run, Pallas kernels for 1% -> 10%
where the time goes in v2:
time: 531 us; the launch traced here: 522 us
  waiting for transfers between devices  232 us (44%)
  Pallas kernels  80.4 us (15%)
  starting transfers between devices  63.5 us (12%)
  other arithmetic  44.4 us (8%)
  matrix products  35.8 us (7%)
  local copies, waits for them, and re-layouts  35.5 us (7%)
  between operations  15.6 us (3%)
  blocking collectives  14.3 us (3%)
    ppermute x6, waiting for transfers between devices, shift(): return lax.ppermute(value, 'wsh', [(i, (i + step) % n) for i in range(n)])  90.9 us
    pallas_call x9, Pallas kernels, call(): pl.pallas_call(kernel, grid=(1,), out_shape=outs, in_specs=in_specs, out_...  80.4 us
    ppermute x9, waiting for transfers between devices, chip_hop(): return lax.ppermute(value, 'chip', [(i, i ^ k) for i in range(n)])  55.1 us
    all_to_all x6, waiting for transfers between devices, exchange(): return lax.all_to_all(value, axis, 0, 0, tiled=True)  53.3 us
    dot_general x6, matrix products, t_dot(): lax.dot_general(a, b, (((0,), (0,)), ((), ())), preferred_element_type=f32)  34.6 us
    all_to_all x6, starting transfers between devices, exchange(): return lax.all_to_all(value, axis, 0, 0, tiled=True)  26.8 us
    all_gather x1, waiting for transfers between devices, body(): held = lax.all_gather(held[None], CTX, axis=0, tiled=True)  25.8 us
    ppermute x6, starting transfers between devices, shift(): return lax.ppermute(value, 'wsh', [(i, (i + step) % n) for i in range(n)])  18.8 us
  transfers between devices with their start and end apart: 34, of which 16 were waited for; matrix products, arithmetic and copies ran while one was open for 14% of the time, Pallas kernels for 10%

profile of v2, /device:TPU:0, one launch (start us, length us, event | category | flops | bytes accessed | tf_op | source)
XLA Modules:
  0.0 521.7 jit_solution(2864605331254700284)
XLA Ops:
  10.2 6.3 %all-to-all-start = ((bf16[4,64,3584]{2,1,0:T(8,128)(2,1)}), bf16[4,64,3584]{2,1,0:T(8,128)(2,1)S(1)}, u32[]{:S(2)}, u32[]{:S(2)}) async-start(bf16[4,64,3584]{2,1,0:T(8,128)(2,1)} %shard_map.263), calls=%async_computation | async-start | bytes 3670016 | tf_op jit(solution)/shard_map/all_to_all | solution.py:381
  26.8 25.1 %collective-permute-done = bf16[16,1536]{1,0:T(8,128)(2,1)S(1)} collective-permute-done((bf16[16,1536]{1,0:T(8,128)(2,1)S(1)}, bf16[16,1536]{1,0:T(8,128)(2,1)S(1)}, u32[]{:S(2)}, u32[]{:S(2)}) %collective-permute-start) | collective-permute-done | bytes 49184 | tf_op jit(solution)/shard_map/ppermute | solution.py:391
  51.9 10.5 %collective-permute-done.1 = bf16[16,1536]{1,0:T(8,128)(2,1)S(1)} collective-permute-done((bf16[16,1536]{1,0:T(8,128)(2,1)S(1)}, bf16[16,1536]{1,0:T(8,128)(2,1)S(1)}, u32[]{:S(2)}, u32[]{:S(2)}) %collective-permute-start.1) | collective-permute-done | bytes 49184 | tf_op jit(solution)/shard_map/ppermute | solution.py:391
  64.6 6.4 %collective-permute-done.5.refs_11_ = bf16[256,2048]{1,0:T(8,128)(2,1)} collective-permute-done((bf16[256,2048]{1,0:T(8,128)(2,1)}, bf16[256,2048]{1,0:T(8,128)(2,1)}, u32[]{:S(2)}, u32[]{:S(2)}) %collective-permute-start.5) | collective-permute-done | bytes 1048608 | tf_op jit(solution)/shard_map/ppermute | solution.py:386
  76.8 11.9 %collective-permute-start.7 = (bf16[128,4096]{1,0:T(8,128)(2,1)S(1)}, bf16[128,4096]{1,0:T(8,128)(2,1)S(1)}, u32[]{:S(2)}, u32[]{:S(2)}) collective-permute-start(bf16[128,4096]{1,0:T(8,128)(2,1)S(1)} %pad_maximum_fusion.1), channel_id=1, source_target_pairs={{0,1},{1,2},{2,3},{3,0},{4,5},{5,6},{6,7},{7,4},{8,9},{9,10},{10,1... | collective-permute-start | bytes 3145736 | tf_op jit(solution)/shard_map/ppermute | solution.py:391
  95.6 16.5 %collective-permute-done.7 = bf16[128,4096]{1,0:T(8,128)(2,1)S(1)} collective-permute-done((bf16[128,4096]{1,0:T(8,128)(2,1)S(1)}, bf16[128,4096]{1,0:T(8,128)(2,1)S(1)}, u32[]{:S(2)}, u32[]{:S(2)}) %collective-permute-start.7) | collective-permute-done | bytes 1048608 | tf_op jit(solution)/shard_map/ppermute | solution.py:391
  116.8 37.4 %collective-permute-done.8 = bf16[128,4096]{1,0:T(8,128)(2,1)S(1)} collective-permute-done((bf16[128,4096]{1,0:T(8,128)(2,1)S(1)}, bf16[128,4096]{1,0:T(8,128)(2,1)S(1)}, u32[]{:S(2)}, u32[]{:S(2)}) %collective-permute-start.8) | collective-permute-done | bytes 1048608 | tf_op jit(solution)/shard_map/ppermute | solution.py:391
  157.8 25.8 %all-gather.3.cloned.1.call-done = bf16[2176,4096]{1,0:T(8,128)(2,1)} async-done(((bf16[272,4096]{1,0:T(8,128)(2,1)}), bf16[2176,4096]{1,0:T(8,128)(2,1)}) %all-gather.3.cloned.1.call-update) | async-done | bytes 17825808 | tf_op jit(solution)/shard_map/all_gather | solution.py:484
  190.3 11.2 %shard_map.264 = (bf16[4,2,128,1024]{3,2,1,0:T(8,128)(2,1)}, bf16[512,2048]{1,0:T(8,128)(2,1)}, bf16[512,2048]{1,0:T(8,128)(2,1)}) custom-call(s32[1]{0:T(128)} %bitcast.1.refs_0_, bf16[512,4096]{1,0:T(8,128)(2,1)} %bitcast.15.refs_1_, f32[1,2048]{1,0:T(1,128)} %reshape.362.refs_2_, f32[1,2048]{1,0:T(1,128)} %reshape.363.refs_3_, ...), custom_call_target="tpu_custom_call" | custom-call | flops 4294967296 | bytes 19945472 | tf_op jit(solution)/shard_map/pallas_call | solution.py:97
  213.7 24.2 %shard_map.265 = (bf16[512,2048]{1,0:T(8,128)(2,1)}, bf16[512,2048]{1,0:T(8,128)(2,1)}, bf16[512,2048]{1,0:T(8,128)(2,1)}, f32[512,2048]{1,0:T(8,128)}, f32[1,2048]{1,0:T(1,128)}) custom-call(s32[1]{0:T(128)} %bitcast.1.refs_0_, bf16[512,4096]{1,0:T(8,128)(2,1)} %bitcast.15.refs_1_, f32[1,2048]{1,0:T(1,128)} %reshape.365.refs_2_, ...), custom_call_target="tpu_custom_call" | custom-call | flops 12884901888 | bytes 32014336 | tf_op jit(solution)/shard_map/pallas_call | solution.py:97
  239.2 9.9 %shard_map.266 = bf16[1024,1024]{1,0:T(8,128)(2,1)} custom-call(bf16[1024,1024]{1,0:T(8,128)(2,1)} %bitcast.154, s32[1024,2]{1,0:T(8,128)} %copy.60.row_ref, s32[1,1024]{1,0:T(1,128)} %bitcast.163, f32[1024,128]{1,0:T(8,128)} %get-tuple-element.155.cos_ref, f32[1024,128]{1,0:T(8,128)} %get-tuple-element.156.sin_ref), custom_call_target="tpu_custom_call" | custom-call | flops 3221225472 | bytes 5255168 | tf_op jit(solution)/shard_map/pallas_call | solution.py:97
  249.1 4.4 convolution_convert_fusion.2
  253.9 7.1 %collective-permute-done.14 = bf16[1024,2048]{1,0:T(8,128)(2,1)} collective-permute-done((bf16[1024,2048]{1,0:T(8,128)(2,1)}, bf16[1024,2048]{1,0:T(8,128)(2,1)}, u32[]{:S(2)}, u32[]{:S(2)}) %collective-permute-start.14) | collective-permute-done | bytes 4194336 | tf_op jit(solution)/shard_map/ppermute | solution.py:377
  261.0 6.8 %convolution_convert_fusion = bf16[2048,2048]{1,0:T(8,128)(2,1)S(1)} fusion(bf16[512,2048]{1,0:T(8,128)(2,1)S(1)} %copy-done.37, bf16[512,4096]{1,0:T(8,128)(2,1)} %bitcast.15.refs_1_), kind=kOutput, calls=%fused_computation.3 | convolution fusion | flops 4299161600 | bytes 12582912 | tf_op jit(solution)/shard_map/dot_general | solution.py:29
  276.7 7.6 %add_convert_fusion = bf16[1024,2048]{1,0:T(8,128)(2,1)} fusion(bf16[1024,2048]{1,0:T(8,128)(2,1)} %collective-permute-done.14, bf16[512,2048]{1,0:T(8,128)(2,1)} %get-tuple-element.101.refs_0_, bf16[512,2048]{1,0:T(8,128)(2,1)} %get-tuple-element.90), kind=kOutput, calls=%fused_computation.2 | convolution fusion | flops 2153775104 | bytes 11534336 | tf_op jit(solution)/shard_map/dot_general | solution.py:29
  284.4 6.1 %fusion = bf16[4,256,2048]{2,1,0:T(8,128)(2,1)} fusion(bf16[4,256,2048]{2,1,0:T(8,128)(2,1)} %collective-permute-done.15, bf16[4,2,256,2048]{3,2,1,0:T(8,128)(2,1)S(1)} %bitcast.144, s32[]{:T(128)S(6)} %select_n.185), kind=kLoop, calls=%fused_computation.1 | loop fusion | flops 8388608 | bytes 12582916 | tf_op jit(solution)/shard_map/convert_element_type | solution.py:409
  290.5 12.8 %all-to-all-done.2 = bf16[8,128,1024]{2,1,0:T(8,128)(2,1)S(1)} async-done(((bf16[8,128,1024]{2,1,0:T(8,128)(2,1)}), bf16[8,128,1024]{2,1,0:T(8,128)(2,1)S(1)}, u32[]{:S(2)}, u32[]{:S(2)}) %all-to-all-start.2) | async-done | bytes 2097184 | tf_op jit(solution)/shard_map/all_to_all | solution.py:381
  307.7 5.4 %convolution_convert_fusion.1 = bf16[1024,1536]{1,0:T(8,128)(2,1)} fusion(bf16[512,1536]{1,0:T(8,128)(2,1)} %get-tuple-element.94.refs_0_, bf16[512,2048]{1,0:T(8,128)(2,1)} %get-tuple-element.100), kind=kOutput, calls=%fused_computation.9 | convolution fusion | flops 1612185600 | bytes 5767168 | tf_op jit(solution)/shard_map/dot_general | solution.py:29
  317.3 5.2 all-to-all-start.3
  322.5 6.0 %add_convert_fusion.1 = bf16[1024,1536]{1,0:T(8,128)(2,1)} fusion(bf16[1024,1536]{1,0:T(8,128)(2,1)} %collective-permute-done.16, bf16[512,1536]{1,0:T(8,128)(2,1)S(1)} %copy-done.13, bf16[512,2048]{1,0:T(8,128)(2,1)} %get-tuple-element.100), kind=kOutput, calls=%fused_computation.4 | convolution fusion | flops 1615331328 | bytes 8912896 | tf_op jit(solution)/shard_map/dot_general | solution.py:29
  328.5 12.4 %shard_map.268 = (f32[512,2048]{1,0:T(8,128)}, f32[2,2048]{1,0:T(2,128)}) custom-call(bf16[512,2048]{1,0:T(8,128)(2,1)} %get-tuple-element.101.refs_0_, bf16[512,4096]{1,0:T(8,128)(2,1)} %bitcast.15.refs_1_, f32[1,2048]{1,0:T(1,128)} %reshape.365.refs_2_, bf16[8,272,4096]{2,1,0:T(8,128)(2,1)} %bitcast.135, bf16[8,272,4096]{2,1,0:T(8,128)(2,1)} %bitcast.136, ...), custom_call_target="tpu_custom_call" | custom-call | flops 4294967296 | bytes 19423232 | tf_op jit(solution)/shard_map/pallas_call | solution.py:97
  340.9 29.9 %all-to-all-done.3 = bf16[4,256,2048]{2,1,0:T(8,128)(2,1)} async-done(((bf16[4,256,2048]{2,1,0:T(8,128)(2,1)}), bf16[4,256,2048]{2,1,0:T(8,128)(2,1)}, u32[]{:S(2)}, u32[]{:S(2)}) %all-to-all-start.3) | async-done | bytes 4194336 | tf_op jit(solution)/shard_map/all_to_all | solution.py:381
  374.6 4.4 convolution_convert_fusion.3
  378.9 10.8 %shard_map.269 = (bf16[512,2048]{1,0:T(8,128)(2,1)}, f32[2,2048]{1,0:T(2,128)}) custom-call(bf16[512,1536]{1,0:T(8,128)(2,1)} %get-tuple-element.94.refs_0_, bf16[512,4096]{1,0:T(8,128)(2,1)} %bitcast.15.refs_1_, f32[1,2048]{1,0:T(1,128)} %reshape.362.refs_2_, bf16[8,272,4096]{2,1,0:T(8,128)(2,1)} %bitcast.139, bf16[8,272,4096]{2,1,0:T(8,128)(2,1)} %bitcast.140, ...), custom_call_target="tpu_custom_call" | custom-call | flops 3221225472 | bytes 18767872 | tf_op jit(solution)/shard_map/pallas_call | solution.py:97
  393.1 4.3 reduce_sum.82
  400.2 10.5 %all-to-all-done.4 = bf16[4,256,1536]{2,1,0:T(8,128)(2,1)S(1)} async-done(((bf16[4,256,1536]{2,1,0:T(8,128)(2,1)}), bf16[4,256,1536]{2,1,0:T(8,128)(2,1)S(1)}, u32[]{:S(2)}, u32[]{:S(2)}) %all-to-all-start.4) | async-done | bytes 3145760 | tf_op jit(solution)/shard_map/all_to_all | solution.py:381
  415.3 14.3 %all_to_all.39 = f32[32,1,768]{2,1,0:T(1,128)S(1)} all-to-all(f32[32,1,768]{2,1,0:T(1,128)S(1)} %copy.67), channel_id=1, replica_groups=mesh['chip'=4,'core'=2,'wsh'=4] {'chip','core','wsh'}, dimensions={0} | all-to-all | bytes 196608 | tf_op jit(solution)/shard_map/all_to_all | solution.py:381
  429.6 3.9 all-to-all-start.5
  445.2 4.9 collective-permute-done.22
  455.5 20.8 %collective-permute-done.20 = bf16[256,2048]{1,0:T(8,128)(2,1)} collective-permute-done((bf16[256,2048]{1,0:T(8,128)(2,1)}, bf16[256,2048]{1,0:T(8,128)(2,1)}, u32[]{:S(2)}, u32[]{:S(2)}) %collective-permute-start.20) | collective-permute-done | bytes 1048608 | tf_op jit(solution)/shard_map/ppermute | solution.py:386
  476.3 20.2 %collective-permute-done.19 = bf16[256,2048]{1,0:T(8,128)(2,1)} collective-permute-done((bf16[256,2048]{1,0:T(8,128)(2,1)}, bf16[256,2048]{1,0:T(8,128)(2,1)}, u32[]{:S(2)}, u32[]{:S(2)}) %collective-permute-start.19) | collective-permute-done | bytes 1048608 | tf_op jit(solution)/shard_map/ppermute | solution.py:386
  498.8 4.2 fusion.4
  (239 shorter events, 119.0 us)
Async XLA Ops:
  10.2 60.9 %all-to-all-start = ((bf16[4,64,3584]{2,1,0:T(8,128)(2,1)}), bf16[4,64,3584]{2,1,0:T(8,128)(2,1)S(1)}, u32[]{:S(2)}, u32[]{:S(2)}) async-start(bf16[4,64,3584]{2,1,0:T(8,128)(2,1)} %shard_map.263), calls=%async_computation | async-start | bytes 3670016 | tf_op jit(solution)/shard_map/all_to_all | solution.py:381
  16.5 167.0 %all-gather.3.cloned.1.call-start = ((), (), s32[]{:S(2)}) async-start(), calls=%async_computation.11 | async-start | bytes 20054016 | tf_op jit(solution)/shard_map/all_gather | solution.py:484
  17.4 34.5 %collective-permute-start = (bf16[16,1536]{1,0:T(8,128)(2,1)S(1)}, bf16[16,1536]{1,0:T(8,128)(2,1)S(1)}, u32[]{:S(2)}, u32[]{:S(2)}) collective-permute-start(bf16[16,1536]{1,0:T(8,128)(2,1)S(1)} %broadcast_in_dim.122), channel_id=1, source_target_pairs={{0,1},{1,2},{2,3},{3,0},{4,5},{5,6},{6,7},{7,4},{8,9},{9,10},{10,1... | collective-permute-start | bytes 147464 | tf_op jit(solution)/shard_map/ppermute | solution.py:391
  19.5 42.9 %collective-permute-start.1 = (bf16[16,1536]{1,0:T(8,128)(2,1)S(1)}, bf16[16,1536]{1,0:T(8,128)(2,1)S(1)}, u32[]{:S(2)}, u32[]{:S(2)}) collective-permute-start(bf16[16,1536]{1,0:T(8,128)(2,1)S(1)} %broadcast_in_dim.122), channel_id=1, source_target_pairs={{0,2},{1,3},{2,0},{3,1},{4,6},{5,7},{6,4},{7,5},{8,10},{9,11},{10,... | collective-permute-start | bytes 147464 | tf_op jit(solution)/shard_map/ppermute | solution.py:391
  21.9 42.8 %collective-permute-start.4 = (bf16[256,2048]{1,0:T(8,128)(2,1)}, bf16[256,2048]{1,0:T(8,128)(2,1)}, u32[]{:S(2)}, u32[]{:S(2)}) collective-permute-start(bf16[256,2048]{1,0:T(8,128)(2,1)} %refs_9_), channel_id=1, source_target_pairs={{0,8},{8,0},{16,24},{24,16},{1,9},{9,1},{17,25},{25,17},{2,10},{10... | collective-permute-start | bytes 3145736 | tf_op jit(solution)/shard_map/ppermute | solution.py:386
  23.4 47.7 %collective-permute-start.5 = (bf16[256,2048]{1,0:T(8,128)(2,1)}, bf16[256,2048]{1,0:T(8,128)(2,1)}, u32[]{:S(2)}, u32[]{:S(2)}) collective-permute-start(bf16[256,2048]{1,0:T(8,128)(2,1)} %refs_9_), channel_id=1, source_target_pairs={{0,16},{8,24},{16,0},{24,8},{1,17},{9,25},{17,1},{25,9},{2,18},{10... | collective-permute-start | bytes 3145736 | tf_op jit(solution)/shard_map/ppermute | solution.py:386
  24.9 46.2 %collective-permute-start.6 = (bf16[256,2048]{1,0:T(8,128)(2,1)}, bf16[256,2048]{1,0:T(8,128)(2,1)}, u32[]{:S(2)}, u32[]{:S(2)}) collective-permute-start(bf16[256,2048]{1,0:T(8,128)(2,1)} %refs_9_), channel_id=1, source_target_pairs={{0,24},{8,16},{16,8},{24,0},{1,25},{9,17},{17,9},{25,1},{2,26},{10... | collective-permute-start | bytes 3145736 | tf_op jit(solution)/shard_map/ppermute | solution.py:386
  51.9 12.5 %collective-permute-start.2 = (bf16[16,1536]{1,0:T(8,128)(2,1)S(1)}, bf16[16,1536]{1,0:T(8,128)(2,1)S(1)}, u32[]{:S(2)}, u32[]{:S(2)}) collective-permute-start(bf16[16,1536]{1,0:T(8,128)(2,1)S(1)} %broadcast_in_dim.122), channel_id=1, source_target_pairs={{0,3},{1,0},{2,1},{3,2},{4,7},{5,4},{6,5},{7,6},{8,11},{9,8},{10,9... | collective-permute-start | bytes 147464 | tf_op jit(solution)/shard_map/ppermute | solution.py:391
  76.8 35.4 %collective-permute-start.7 = (bf16[128,4096]{1,0:T(8,128)(2,1)S(1)}, bf16[128,4096]{1,0:T(8,128)(2,1)S(1)}, u32[]{:S(2)}, u32[]{:S(2)}) collective-permute-start(bf16[128,4096]{1,0:T(8,128)(2,1)S(1)} %pad_maximum_fusion.1), channel_id=1, source_target_pairs={{0,1},{1,2},{2,3},{3,0},{4,5},{5,6},{6,7},{7,4},{8,9},{9,10},{10,1... | collective-permute-start | bytes 3145736 | tf_op jit(solution)/shard_map/ppermute | solution.py:391
  88.7 65.5 %collective-permute-start.8 = (bf16[128,4096]{1,0:T(8,128)(2,1)S(1)}, bf16[128,4096]{1,0:T(8,128)(2,1)S(1)}, u32[]{:S(2)}, u32[]{:S(2)}) collective-permute-start(bf16[128,4096]{1,0:T(8,128)(2,1)S(1)} %pad_maximum_fusion.1), channel_id=1, source_target_pairs={{0,2},{1,3},{2,0},{3,1},{4,6},{5,7},{6,4},{7,5},{8,10},{9,11},{10,... | collective-permute-start | bytes 3145736 | tf_op jit(solution)/shard_map/ppermute | solution.py:391
  88.7 68.0 %collective-permute-start.9 = (bf16[128,4096]{1,0:T(8,128)(2,1)S(1)}, bf16[128,4096]{1,0:T(8,128)(2,1)S(1)}, u32[]{:S(2)}, u32[]{:S(2)}) collective-permute-start(bf16[128,4096]{1,0:T(8,128)(2,1)S(1)} %pad_maximum_fusion.1), channel_id=1, source_target_pairs={{0,3},{1,0},{2,1},{3,2},{4,7},{5,4},{6,5},{7,6},{8,11},{9,8},{10,9... | collective-permute-start | bytes 3145736 | tf_op jit(solution)/shard_map/ppermute | solution.py:391
  91.1 66.6 %collective-permute-start.10 = (bf16[256,2048]{1,0:T(8,128)(2,1)S(1)}, bf16[256,2048]{1,0:T(8,128)(2,1)S(1)}, u32[]{:S(2)}, u32[]{:S(2)}) collective-permute-start(bf16[256,2048]{1,0:T(8,128)(2,1)S(1)} %copy-done.14), channel_id=1, source_target_pairs={{0,4},{4,0},{1,5},{5,1},{2,6},{6,2},{3,7},{7,3},{8,12},{12,8},{9,1... | collective-permute-start | bytes 3145736 | tf_op jit(solution)/shard_map/ppermute | solution.py:377
  92.1 65.6 %collective-permute-start.11 = (bf16[256,2048]{1,0:T(8,128)(2,1)}, bf16[256,2048]{1,0:T(8,128)(2,1)}, u32[]{:S(2)}, u32[]{:S(2)}) collective-permute-start(bf16[256,2048]{1,0:T(8,128)(2,1)} %collective-permute-done.4.refs_10_), channel_id=1, source_target_pairs={{0,4},{4,0},{1,5},{5,1},{2,6},{6,2},{3,7},{7,3},{8,12},{12,8},{9,1... | collective-permute-start | bytes 3145736 | tf_op jit(solution)/shard_map/ppermute | solution.py:377
  112.1 45.6 %collective-permute-start.12 = (bf16[256,2048]{1,0:T(8,128)(2,1)}, bf16[256,2048]{1,0:T(8,128)(2,1)}, u32[]{:S(2)}, u32[]{:S(2)}) collective-permute-start(bf16[256,2048]{1,0:T(8,128)(2,1)} %collective-permute-done.5.refs_11_), channel_id=1, source_target_pairs={{0,4},{4,0},{1,5},{5,1},{2,6},{6,2},{3,7},{7,3},{8,12},{12,8},{9,1... | collective-permute-start | bytes 3145736 | tf_op jit(solution)/shard_map/ppermute | solution.py:377
  154.2 3.6 collective-permute-start.13
  201.5 36.4 %all-to-all-start.1 = ((bf16[8,128,1024]{2,1,0:T(8,128)(2,1)}), bf16[8,128,1024]{2,1,0:T(8,128)(2,1)S(1)}, u32[]{:S(2)}, u32[]{:S(2)}) async-start(bf16[8,128,1024]{2,1,0:T(8,128)(2,1)} %bitcast.153), calls=%async_computation.1 | async-start | bytes 4194304 | tf_op jit(solution)/shard_map/all_to_all | solution.py:381
  253.5 7.5 %collective-permute-start.14 = (bf16[1024,2048]{1,0:T(8,128)(2,1)}, bf16[1024,2048]{1,0:T(8,128)(2,1)}, u32[]{:S(2)}, u32[]{:S(2)}) collective-permute-start(bf16[1024,2048]{1,0:T(8,128)(2,1)} %convolution_convert_fusion.2), channel_id=1, source_target_pairs={{0,4},{4,0},{1,5},{5,1},{2,6},{6,2},{3,7},{7,3},{8,12},{12,8},{9,1... | collective-permute-start | bytes 12582920 | tf_op jit(solution)/shard_map/ppermute | solution.py:377
  272.4 12.0 %collective-permute-start.15 = (bf16[4,256,2048]{2,1,0:T(8,128)(2,1)}, bf16[4,256,2048]{2,1,0:T(8,128)(2,1)}, u32[]{:S(2)}, u32[]{:S(2)}) collective-permute-start(bf16[4,256,2048]{2,1,0:T(8,128)(2,1)} %dynamic-slice_bitcast_fusion), channel_id=1, source_target_pairs={{0,4},{4,0},{1,5},{5,1},{2,6},{6,2},{3,7},{7,3},{8,12},{12,8},{9,1... | collective-permute-start | bytes 12582920 | tf_op jit(solution)/shard_map/ppermute | solution.py:377
  272.8 30.5 %all-to-all-start.2 = ((bf16[8,128,1024]{2,1,0:T(8,128)(2,1)}), bf16[8,128,1024]{2,1,0:T(8,128)(2,1)S(1)}, u32[]{:S(2)}, u32[]{:S(2)}) async-start(bf16[8,128,1024]{2,1,0:T(8,128)(2,1)} %bitcast.155), calls=%async_computation.2 | async-start | bytes 4194304 | tf_op jit(solution)/shard_map/all_to_all | solution.py:381
  276.7 113.1 %reduce-scatter.3.cloned.1.call-start = ((), (), s32[]{:S(2)}) async-start(), calls=%async_computation.9 | async-start | bytes 2621440 | tf_op jit(solution)/shard_map/reduce_scatter | solution.py:532
  313.1 9.4 %collective-permute-start.16 = (bf16[1024,1536]{1,0:T(8,128)(2,1)}, bf16[1024,1536]{1,0:T(8,128)(2,1)}, u32[]{:S(2)}, u32[]{:S(2)}) collective-permute-start(bf16[1024,1536]{1,0:T(8,128)(2,1)} %convolution_convert_fusion.1), channel_id=1, source_target_pairs={{0,4},{4,0},{1,5},{5,1},{2,6},{6,2},{3,7},{7,3},{8,12},{12,8},{9,1... | collective-permute-start | bytes 9437192 | tf_op jit(solution)/shard_map/ppermute | solution.py:377
  317.3 53.5 %all-to-all-start.3 = ((bf16[4,256,2048]{2,1,0:T(8,128)(2,1)}), bf16[4,256,2048]{2,1,0:T(8,128)(2,1)}, u32[]{:S(2)}, u32[]{:S(2)}) async-start(bf16[4,256,2048]{2,1,0:T(8,128)(2,1)} %bitcast.149), calls=%async_computation.3 | async-start | bytes 8388608 | tf_op jit(solution)/shard_map/all_to_all | solution.py:381
  370.8 39.9 %all-to-all-start.4 = ((bf16[4,256,1536]{2,1,0:T(8,128)(2,1)}), bf16[4,256,1536]{2,1,0:T(8,128)(2,1)S(1)}, u32[]{:S(2)}, u32[]{:S(2)}) async-start(bf16[4,256,1536]{2,1,0:T(8,128)(2,1)} %bitcast.150), calls=%async_computation.6 | async-start | bytes 6291456 | tf_op jit(solution)/shard_map/all_to_all | solution.py:381
  374.5 135.5 %reduce-scatter.5.cloned.1.call-start = ((), (), s32[]{:S(2)}) async-start(), calls=%async_computation.10 | async-start | bytes 2621440 | tf_op jit(solution)/shard_map/reduce_scatter | solution.py:540
  392.1 5.2 collective-permute-start.17
  429.6 73.3 %all-to-all-start.5 = ((bf16[4,64,3584]{2,1,0:T(8,128)(2,1)}), bf16[4,64,3584]{2,1,0:T(8,128)(2,1)S(1)}, u32[]{:S(2)}, u32[]{:S(2)}) async-start(bf16[4,64,3584]{2,1,0:T(8,128)(2,1)} %bitcast.146), calls=%async_computation.7 | async-start | bytes 3670016 | tf_op jit(solution)/shard_map/all_to_all | solution.py:381
  434.3 10.1 %collective-permute-start.23 = (bf16[64,2048]{1,0:T(8,128)(2,1)S(1)}, bf16[64,2048]{1,0:T(8,128)(2,1)S(1)}, u32[]{:S(2)}, u32[]{:S(2)}) collective-permute-start(bf16[64,2048]{1,0:T(8,128)(2,1)S(1)} %get-tuple-element.134), channel_id=1, source_target_pairs={{0,24},{8,16},{16,8},{24,0},{1,25},{9,17},{17,9},{25,1},{2,26},{10... | collective-permute-start | bytes 786440 | tf_op jit(solution)/shard_map/ppermute | solution.py:386
  435.7 14.4 %collective-permute-start.22 = (bf16[64,2048]{1,0:T(8,128)(2,1)}, bf16[64,2048]{1,0:T(8,128)(2,1)}, u32[]{:S(2)}, u32[]{:S(2)}) collective-permute-start(bf16[64,2048]{1,0:T(8,128)(2,1)} %get-tuple-element.135), channel_id=1, source_target_pairs={{0,16},{8,24},{16,0},{24,8},{1,17},{9,25},{17,1},{25,9},{2,18},{10... | collective-permute-start | bytes 786440 | tf_op jit(solution)/shard_map/ppermute | solution.py:386
  436.8 13.3 %collective-permute-start.21 = (bf16[64,2048]{1,0:T(8,128)(2,1)S(1)}, bf16[64,2048]{1,0:T(8,128)(2,1)}, u32[]{:S(2)}, u32[]{:S(2)}) collective-permute-start(bf16[64,2048]{1,0:T(8,128)(2,1)S(1)} %get-tuple-element.133), channel_id=1, source_target_pairs={{0,8},{8,0},{16,24},{24,16},{1,9},{9,1},{17,25},{25,17},{2,10},{10... | collective-permute-start | bytes 786440 | tf_op jit(solution)/shard_map/ppermute | solution.py:386
  441.4 34.9 %collective-permute-start.20 = (bf16[256,2048]{1,0:T(8,128)(2,1)}, bf16[256,2048]{1,0:T(8,128)(2,1)}, u32[]{:S(2)}, u32[]{:S(2)}) collective-permute-start(bf16[256,2048]{1,0:T(8,128)(2,1)} %get-tuple-element.131), channel_id=1, source_target_pairs={{0,24},{8,16},{16,8},{24,0},{1,25},{9,17},{17,9},{25,1},{2,26},{10... | collective-permute-start | bytes 3145736 | tf_op jit(solution)/shard_map/ppermute | solution.py:386
  442.8 53.7 %collective-permute-start.19 = (bf16[256,2048]{1,0:T(8,128)(2,1)}, bf16[256,2048]{1,0:T(8,128)(2,1)}, u32[]{:S(2)}, u32[]{:S(2)}) collective-permute-start(bf16[256,2048]{1,0:T(8,128)(2,1)} %get-tuple-element.132), channel_id=1, source_target_pairs={{0,16},{8,24},{16,0},{24,8},{1,17},{9,25},{17,1},{25,9},{2,18},{10... | collective-permute-start | bytes 3145736 | tf_op jit(solution)/shard_map/ppermute | solution.py:386
  444.4 54.3 %collective-permute-start.18 = (bf16[256,2048]{1,0:T(8,128)(2,1)}, bf16[256,2048]{1,0:T(8,128)(2,1)}, u32[]{:S(2)}, u32[]{:S(2)}) collective-permute-start(bf16[256,2048]{1,0:T(8,128)(2,1)} %get-tuple-element.130), channel_id=1, source_target_pairs={{0,8},{8,0},{16,24},{24,16},{1,9},{9,1},{17,25},{25,17},{2,10},{10... | collective-permute-start | bytes 3145736 | tf_op jit(solution)/shard_map/ppermute | solution.py:386
  (41 other events, 447.5 us)
Sparse Core Ops, SparseCore 0:
  76.7 106.8 all-gather.2
  317.4 43.6 reduce-scatter.2
  392.3 47.4 reduce-scatter.4

commit v3 on v2

--- a/solution.py
+++ b/solution.py
@@ -79,7 +79,6 @@
 
 
 def call(kernel, outs, operands, flops, scratch=(), scalar=None):
-    moved = sum(o.size * o.dtype.itemsize for o in list(operands) + list(outs))
     in_specs, arrays = [], []
     if scalar is not None:
         in_specs.append(pl.BlockSpec(memory_space=pltpu.SMEM))
@@ -102,7 +101,7 @@
         out_specs=out_specs,
         scratch_shapes=list(scratch),
         compiler_params=pltpu.CompilerParams(vmem_limit_bytes=VMEM_LIMIT),
-        cost_estimate=pl.CostEstimate(flops=flops, bytes_accessed=moved, transcendentals=0),
+        cost_estimate=pl.CostEstimate(flops=0, bytes_accessed=0, transcendentals=0),
     )(*arrays)
 
 
@@ -164,15 +163,16 @@
         out_ref[rows, 3 * hd : 4 * hd] = dv_ref[rows, :].astype(bf16)
 
 
-def attention(packed, places, cut):
+def attention_tables(places, cut):
+    cos_table, sin_table = rotary_tables(places, -1.0)
+    return jnp.stack([places, jnp.where(places >= cut, cut, 0)], 1), places[None, :], cos_table, sin_table
+
+
+def attention(packed, *tables):
     length = packed.shape[0]
-    cos_table, sin_table = rotary_tables(places, -1.0)
-    first = jnp.where(places >= cut, cut, 0)
-    row_info = jnp.stack([places, first], 1)
-    operands = (packed, row_info, places[None, :], cos_table, sin_table)
     scratch = [pltpu.VMEM((length, HEAD_DIM), f32), pltpu.VMEM((length, HEAD_DIM), f32)]
     outs = [shaped((length, 4 * HEAD_DIM), bf16)]
-    return call(attention_kernel, outs, operands, 12 * length * length * HEAD_DIM, scratch)[0]
+    return call(attention_kernel, outs, (packed, *tables), 12 * length * length * HEAD_DIM, scratch)[0]
 
 
 def project(acts, gain, shift_by, held, bias, cos, sin, part, tokens, index):
@@ -403,10 +403,13 @@
     return jnp.sum(value.astype(f32), 0).astype(bf16)
 
 
-def over_cores(value):
-    core = lax.axis_index("core")
-    away = hop(lax.dynamic_index_in_dim(value, 1 - core, 1, False))
-    return (lax.dynamic_index_in_dim(value, core, 1, False).astype(f32) + away.astype(f32)).astype(bf16)
+def over_cores_send(value):
+    return hop(lax.dynamic_index_in_dim(value, 1 - lax.axis_index("core"), 1, False))
+
+
+def over_cores_add(value, away):
+    kept = lax.dynamic_index_in_dim(value, lax.axis_index("core"), 1, False)
+    return (kept.astype(f32) + away.astype(f32)).astype(bf16)
 
 
 def hop_terms(terms):
@@ -501,6 +504,10 @@
 
     own_places = block_places(lax.dynamic_index_in_dim(orders, c, 1, False), C, T).reshape(-1)
     own_cos, own_sin = rotary_tables(own_places, 1.0)
+    seq = c // R // HL
+    seq_order = lax.dynamic_index_in_dim(orders, seq, 0, False)
+    seq_cut = lax.dynamic_index_in_dim(cuts, seq, 0, False)
+    tables = attention_tables(block_places(seq_order, C, T).reshape(-1), seq_cut)
     send, h_attn, full_dense = project(acts, ga, sa, held, bias_qkv, own_cos, own_sin, PART, T, c)
     send = send.reshape(PAIRS, T, 4 * HEAD_DIM)
     if R > 1:
@@ -508,20 +515,16 @@
     packed = exchange(send, CTX).reshape(C * T, 4 * HEAD_DIM)
 
     h_mlp, hidden, d_pre, out_mlp, sum_pre = feed_forward(
-        after(acts, send), gm, sm, held, bias_up, blocks_down, PART, c
+        after(acts, send, *tables), gm, sm, held, bias_up, blocks_down, PART, c
     )
-    seq = c // R // HL
-    seq_order = lax.dynamic_index_in_dim(orders, seq, 0, False)
-    seq_cut = lax.dynamic_index_in_dim(cuts, seq, 0, False)
-    result = attention(after(packed, d_pre), block_places(seq_order, C, T).reshape(-1), seq_cut)
+    result = attention(after(packed, d_pre), *tables)
 
     h_late = after(h_mlp, result)
     result = exchange(result.reshape(C, T, 4 * HEAD_DIM), CTX)
     away_up = hop(t_dot(h_late[:, D // 2 :], d_pre).astype(bf16))
     gw_down = t_dot(after(hidden, away_up), g).astype(bf16)
     kept_up = (t_dot(h_late[:, : D // 2], d_pre) + away_up.astype(f32)).astype(bf16)
-    kept_down = over_cores(gw_down.reshape(C // 2, 2, FL, D))
-    result = after(result, kept_up, kept_down)
+    result = after(result, gw_down, kept_up)
     arrived_up = exchange(after(kept_up, result).reshape(C // 2, PART, C * FL), "chip")
     if R > 1:
         result = result.reshape(PAIRS, R, T, 4 * HEAD_DIM)[:, 0]
@@ -530,25 +533,21 @@
     out_part = (out_mlp + dot(after(attended, away_qkv), full_dense)).astype(bf16)
     away_here = hop(away_qkv)
     out_sum = lax.psum_scatter(out_part.reshape(W * T, D), "wsh", scatter_dimension=0, tiled=True)
-    gw_dense = t_dot(attended, g).astype(bf16)
     kept_qkv = (t_dot(after(h_attn, out_part)[:, : D // 2], d_proj) + away_here.astype(f32)).astype(bf16)
     e_mlp, sums_mlp = input_terms(after(d_pre, kept_qkv), held, 4, acts, gm, PART)
-    e_mlp, arrived_up = lax.optimization_barrier((e_mlp, arrived_up))
-    arrived_qkv = exchange(after(kept_qkv, arrived_up).reshape(C // 2, PART, 3 * E), "chip")
     e_part, sums_attn = input_terms(d_proj, held, 0, acts, ga, PART, e_mlp)
     e_part, out_sum = lax.optimization_barrier((e_part, out_sum))
+    arrived_up = after(arrived_up, e_part)
+    arrived_qkv = exchange(after(kept_qkv, arrived_up).reshape(C // 2, PART, 3 * E), "chip")
     e_sum = lax.psum_scatter(e_part, "wsh", scatter_dimension=0, tiled=True)
 
-    kept_dense = over_cores(after(gw_dense, e_part).reshape(C // 2, 2, DL, D))
-    own_up = sum_arrived(after(arrived_up, e_part))
+    gw_dense = t_dot(after(attended, e_part), g).astype(bf16).reshape(C // 2, 2, DL, D)
+    kept_dense = over_cores_add(gw_dense, over_cores_send(gw_dense))
+    own_up = sum_arrived(arrived_up)
     arrived_qkv = after(arrived_qkv, own_up, kept_dense)
     own_grads = jnp.concatenate([sum_arrived(arrived_qkv), own_up], 1)
     back = exchange(own_grads.reshape(W, DL, 7 * E), "wsh")
-    kept_down = after(kept_down, arrived_qkv)
-    terms = [lax.dynamic_index_in_dim(kept_down, lax.axis_index("chip") ^ k, 0, False) for k in range(C // 2)]
-    grad_down = terms[0].astype(f32)
-    for term in hop_terms(terms):
-        grad_down = grad_down + term.astype(f32)
+    grad_down = lax.psum_scatter(after(gw_down, arrived_qkv), CTX, scatter_dimension=0, tiled=True).astype(f32)
     terms = [lax.dynamic_index_in_dim(kept_dense, lax.axis_index("chip") ^ k, 0, False) for k in range(C // 2)]
     grad_dense = lax.ppermute(sum_terms(terms[0], hop_terms(terms)), both, back_moves).astype(f32)
 
@@ -557,7 +556,7 @@
     input_gradient = (
         cot + (e - jnp.mean(e, -1, keepdims=True) - normed * jnp.mean(e * normed, -1, keepdims=True)) * inv_std
     )
-    grad_qkv = join_qkv(after(back, grad_down), 3 * E)
+    grad_qkv = join_qkv(back, 3 * E)
     grad_up = join_up(back, 3 * E, C)
 
     sum_proj = sum_proj.reshape(HL, 3, HEAD_DIM).transpose(1, 0, 2).reshape(3, 1, E)
@@ -567,7 +566,7 @@
     by_width = jnp.concatenate([sums_attn, sums_mlp, jnp.sum(cot, 0, keepdims=True)], 0)
     by_width = by_width.reshape(5, C * W, DL).transpose(1, 0, 2).reshape(C * W, 5 * DL)
     vectors = jnp.concatenate([gb_up, gb_qkv, by_width], 1)
-    summed = jnp.sum(exchange(after(vectors, own_grads), both), 0)
+    summed = jnp.sum(exchange(after(vectors, back), both), 0)
     n_up, n_qkv = gb_up.shape[1], gb_qkv.shape[1]
     gb_up, gb_qkv = summed[:n_up], summed[n_up : n_up + n_qkv]
     g_ga, g_sa, g_gm, g_sm, gb_dense = [

time: 531 us -> 493 us (0.928)
  waiting for transfers between devices: 232 us -> 206 us
  blocking collectives: 14.3 us -> 0 us
  starting transfers between devices: 63.5 us -> 75.6 us
  other arithmetic: 44.4 us -> 38.7 us
    ppermute x9 -> x6, waiting for transfers between devices: 55.1 us -> 13.8 us  [chip_hop(): return lax.ppermute(value, 'chip', [(i, i ^ k) for i in range(n)])]
    all_gather x1, waiting for transfers between devices: 25.8 us -> 0.01 us  [body(): held = lax.all_gather(held[None], CTX, axis=0, tiled=True)]
    ppermute x6, waiting for transfers between devices: 90.9 us -> 116 us  [shift(): return lax.ppermute(value, 'wsh', [(i, (i + step) % n) for i in range(n)])]
    all_to_all x1 -> x0, blocking collectives: 14.3 us -> none  [exchange(): return lax.all_to_all(value, axis, 0, 0, tiled=True)]
    all_to_all x6 -> x7, starting transfers between devices: 26.8 us -> 38.3 us  [exchange(): return lax.all_to_all(value, axis, 0, 0, tiled=True)]
    all_to_all x6 -> x7, waiting for transfers between devices: 53.3 us -> 64.6 us  [exchange(): return lax.all_to_all(value, axis, 0, 0, tiled=True)]
    squeeze x3 -> x1, local copies, waits for them, and re-layouts: 8.87 us -> 0.07 us  [over_cores_send(): lax.dynamic_index_in_dim(value, 1 - lax.axis_index('core'), 1, False)]
    reduce_scatter x1, waiting for transfers between devices: 0.02 us -> 8.01 us  [body(): lax.psum_scatter(out_part.reshape(W * T, D), 'wsh', scatter_dimension=0,...]
  transfers between devices with their start and end apart: 34 -> 32, of which waited for: 16 -> 15; matrix products, arithmetic and copies ran while one was open for 14% -> 14% of each run, Pallas kernels for 10% -> 11%
where the time goes in v3:
time: 493 us; the launch traced here: 485 us
  waiting for transfers between devices  206 us (42%)
  Pallas kernels  80 us (16%)
  starting transfers between devices  75.6 us (15%)
  other arithmetic  38.7 us (8%)
  matrix products  35.8 us (7%)
  local copies, waits for them, and re-layouts  33.3 us (7%)
  between operations  15.6 us (3%)
    ppermute x6, waiting for transfers between devices, shift(): return lax.ppermute(value, 'wsh', [(i, (i + step) % n) for i in range(n)])  116 us
    pallas_call x9, Pallas kernels, call(): pl.pallas_call(kernel, grid=(1,), out_shape=outs, in_specs=in_specs, out_...  80 us
    all_to_all x7, waiting for transfers between devices, exchange(): return lax.all_to_all(value, axis, 0, 0, tiled=True)  64.6 us
    all_to_all x7, starting transfers between devices, exchange(): return lax.all_to_all(value, axis, 0, 0, tiled=True)  38.3 us
    dot_general x6, matrix products, t_dot(): lax.dot_general(a, b, (((0,), (0,)), ((), ())), preferred_element_type=f32)  34.5 us
    ppermute x6, starting transfers between devices, shift(): return lax.ppermute(value, 'wsh', [(i, (i + step) % n) for i in range(n)])  20.6 us
    ppermute x6, waiting for transfers between devices, chip_hop(): return lax.ppermute(value, 'chip', [(i, i ^ k) for i in range(n)])  13.8 us
    unnamed x69, local copies, waits for them, and re-layouts  10.1 us
  transfers between devices with their start and end apart: 32, of which 15 were waited for; matrix products, arithmetic and copies ran while one was open for 14% of the time, Pallas kernels for 11%

profile of v3, /device:TPU:0, one launch (start us, length us, event | category | flops | bytes accessed | tf_op | source)
XLA Modules:
  0.0 484.8 jit_solution(2095175038303012076)
XLA Ops:
  10.1 6.5 %all-to-all-start = ((bf16[4,64,3584]{2,1,0:T(8,128)(2,1)}), bf16[4,64,3584]{2,1,0:T(8,128)(2,1)S(1)}, u32[]{:S(2)}, u32[]{:S(2)}) async-start(bf16[4,64,3584]{2,1,0:T(8,128)(2,1)} %shard_map.263), calls=%async_computation | async-start | bytes 3670016 | tf_op jit(solution)/shard_map/all_to_all | solution.py:381
  26.9 35.9 %collective-permute-done.1 = bf16[16,1536]{1,0:T(8,128)(2,1)S(1)} collective-permute-done((bf16[16,1536]{1,0:T(8,128)(2,1)S(1)}, bf16[16,1536]{1,0:T(8,128)(2,1)S(1)}, u32[]{:S(2)}, u32[]{:S(2)}) %collective-permute-start.1) | collective-permute-done | bytes 49184 | tf_op jit(solution)/shard_map/ppermute | solution.py:391
  72.0 3.1 fusion.1
  76.3 14.2 %collective-permute-start.7 = (bf16[128,4096]{1,0:T(8,128)(2,1)S(1)}, bf16[128,4096]{1,0:T(8,128)(2,1)S(1)}, u32[]{:S(2)}, u32[]{:S(2)}) collective-permute-start(bf16[128,4096]{1,0:T(8,128)(2,1)S(1)} %copy-done.5), channel_id=1, source_target_pairs={{0,1},{1,2},{2,3},{3,0},{4,5},{5,6},{6,7},{7,4},{8,9},{9,10},{10,1... | collective-permute-start | bytes 3145736 | tf_op jit(solution)/shard_map/ppermute | solution.py:391
  97.7 16.2 %collective-permute-done.7 = bf16[128,4096]{1,0:T(8,128)(2,1)S(1)} collective-permute-done((bf16[128,4096]{1,0:T(8,128)(2,1)S(1)}, bf16[128,4096]{1,0:T(8,128)(2,1)S(1)}, u32[]{:S(2)}, u32[]{:S(2)}) %collective-permute-start.7) | collective-permute-done | bytes 1048608 | tf_op jit(solution)/shard_map/ppermute | solution.py:391
  113.9 3.5 collective-permute-start.12
  118.5 62.8 %collective-permute-done.8 = bf16[128,4096]{1,0:T(8,128)(2,1)S(1)} collective-permute-done((bf16[128,4096]{1,0:T(8,128)(2,1)S(1)}, bf16[128,4096]{1,0:T(8,128)(2,1)S(1)}, u32[]{:S(2)}, u32[]{:S(2)}) %collective-permute-start.8) | collective-permute-done | bytes 1048608 | tf_op jit(solution)/shard_map/ppermute | solution.py:391
  193.1 11.2 %shard_map.264 = (bf16[4,2,128,1024]{3,2,1,0:T(8,128)(2,1)}, bf16[512,2048]{1,0:T(8,128)(2,1)}, bf16[512,2048]{1,0:T(8,128)(2,1)}) custom-call(s32[1]{0:T(128)} %bitcast.1.refs_0_, bf16[512,4096]{1,0:T(8,128)(2,1)} %bitcast.15.refs_1_, f32[1,2048]{1,0:T(1,128)} %reshape.354.refs_2_, f32[1,2048]{1,0:T(1,128)} %reshape.355.refs_3_, ...), custom_call_target="tpu_custom_call" | custom-call | tf_op jit(solution)/shard_map/pallas_call | solution.py:96
  204.4 4.1 all-to-all-start.1
  216.8 24.1 %shard_map.265 = (bf16[512,2048]{1,0:T(8,128)(2,1)}, bf16[512,2048]{1,0:T(8,128)(2,1)}, bf16[512,2048]{1,0:T(8,128)(2,1)}, f32[512,2048]{1,0:T(8,128)}, f32[1,2048]{1,0:T(1,128)}) custom-call(s32[1]{0:T(128)} %bitcast.1.refs_0_, bf16[512,4096]{1,0:T(8,128)(2,1)} %bitcast.15.refs_1_, f32[1,2048]{1,0:T(1,128)} %reshape.357.refs_2_, ...), custom_call_target="tpu_custom_call" | custom-call | tf_op jit(solution)/shard_map/pallas_call | solution.py:96
  242.2 9.9 %shard_map.266 = bf16[1024,1024]{1,0:T(8,128)(2,1)} custom-call(bf16[1024,1024]{1,0:T(8,128)(2,1)} %bitcast.126, s32[1024,2]{1,0:T(8,128)} %copy.57.row_ref, s32[1,1024]{1,0:T(1,128)} %bitcast.141, f32[1024,128]{1,0:T(8,128)} %get-tuple-element.146.cos_ref, f32[1024,128]{1,0:T(8,128)} %get-tuple-element.147.sin_ref), custom_call_target="tpu_custom_call" | custom-call | tf_op jit(solution)/shard_map/pallas_call | solution.py:96
  252.1 4.3 convolution_convert_fusion.2
  256.9 3.8 all-to-all-start.2
  264.0 7.6 %add_convert_fusion = bf16[1024,2048]{1,0:T(8,128)(2,1)} fusion(bf16[1024,2048]{1,0:T(8,128)(2,1)} %collective-permute-done.14, bf16[512,2048]{1,0:T(8,128)(2,1)} %get-tuple-element.98.refs_0_, bf16[512,2048]{1,0:T(8,128)(2,1)} %get-tuple-element.88), kind=kOutput, calls=%fused_computation | convolution fusion | flops 2153775104 | bytes 11534336 | tf_op jit(solution)/shard_map/dot_general | solution.py:29
  271.6 8.4 %convolution_convert_fusion = bf16[2048,2048]{1,0:T(8,128)(2,1)} fusion(bf16[512,2048]{1,0:T(8,128)(2,1)S(1)} %copy-done.31, bf16[512,4096]{1,0:T(8,128)(2,1)} %bitcast.15.refs_1_), kind=kOutput, calls=%fused_computation.1 | convolution fusion | flops 4299161600 | bytes 12582912 | tf_op jit(solution)/shard_map/dot_general | solution.py:29
  280.1 7.3 %all-to-all-done.2 = bf16[8,128,1024]{2,1,0:T(8,128)(2,1)S(1)} async-done(((bf16[8,128,1024]{2,1,0:T(8,128)(2,1)}), bf16[8,128,1024]{2,1,0:T(8,128)(2,1)S(1)}, u32[]{:S(2)}, u32[]{:S(2)}) %all-to-all-start.2) | async-done | bytes 2097184 | tf_op jit(solution)/shard_map/all_to_all | solution.py:381
  291.7 5.4 %convolution_convert_fusion.1 = bf16[1024,1536]{1,0:T(8,128)(2,1)} fusion(bf16[512,1536]{1,0:T(8,128)(2,1)} %get-tuple-element.91.refs_0_, bf16[512,2048]{1,0:T(8,128)(2,1)} %get-tuple-element.97), kind=kOutput, calls=%fused_computation.6 | convolution fusion | flops 1612185600 | bytes 5767168 | tf_op jit(solution)/shard_map/dot_general | solution.py:29
  301.4 5.0 %all-to-all-start.3 = ((bf16[4,256,2048]{2,1,0:T(8,128)(2,1)}), bf16[4,256,2048]{2,1,0:T(8,128)(2,1)}, u32[]{:S(2)}, u32[]{:S(2)}) async-start(bf16[4,256,2048]{2,1,0:T(8,128)(2,1)} %bitcast.131), calls=%async_computation.5 | async-start | bytes 8388608 | tf_op jit(solution)/shard_map/all_to_all | solution.py:381
  307.4 5.8 %add_convert_fusion.1 = bf16[1024,1536]{1,0:T(8,128)(2,1)} fusion(bf16[1024,1536]{1,0:T(8,128)(2,1)} %collective-permute-done.15, bf16[512,1536]{1,0:T(8,128)(2,1)S(1)} %copy-done.11, bf16[512,2048]{1,0:T(8,128)(2,1)} %get-tuple-element.97), kind=kOutput, calls=%fused_computation.2 | convolution fusion | flops 1615331328 | bytes 8912896 | tf_op jit(solution)/shard_map/dot_general | solution.py:29
  313.2 12.2 %shard_map.268 = (f32[512,2048]{1,0:T(8,128)}, f32[2,2048]{1,0:T(2,128)}) custom-call(bf16[512,2048]{1,0:T(8,128)(2,1)} %get-tuple-element.98.refs_0_, bf16[512,4096]{1,0:T(8,128)(2,1)} %bitcast.15.refs_1_, f32[1,2048]{1,0:T(1,128)} %reshape.357.refs_2_, bf16[8,272,4096]{2,1,0:T(8,128)(2,1)} %bitcast.118, bf16[8,272,4096]{2,1,0:T(8,128)(2,1)} %bitcast.119, ...), custom_call_target="tpu_custom_call" | custom-call | tf_op jit(solution)/shard_map/pallas_call | solution.py:96
  325.4 10.9 %shard_map.269 = (bf16[512,2048]{1,0:T(8,128)(2,1)}, f32[2,2048]{1,0:T(2,128)}) custom-call(bf16[512,1536]{1,0:T(8,128)(2,1)} %get-tuple-element.91.refs_0_, bf16[512,4096]{1,0:T(8,128)(2,1)} %bitcast.15.refs_1_, f32[1,2048]{1,0:T(1,128)} %reshape.354.refs_2_, bf16[8,272,4096]{2,1,0:T(8,128)(2,1)} %bitcast.122, bf16[8,272,4096]{2,1,0:T(8,128)(2,1)} %bitcast.123, ...), custom_call_target="tpu_custom_call" | custom-call | tf_op jit(solution)/shard_map/pallas_call | solution.py:96
  336.3 8.0 %reduce-scatter.4.cloned.1.call-done = bf16[128,2048]{1,0:T(8,128)(2,1)} async-done(((bf16[512,2048]{1,0:T(8,128)(2,1)}), bf16[128,2048]{1,0:T(8,128)(2,1)}) %reduce-scatter.4.cloned.1.call-update) | async-done | bytes 524304 | tf_op jit(solution)/shard_map/reduce_scatter | solution.py:535
  344.4 10.4 %all-to-all-done.3 = bf16[4,256,2048]{2,1,0:T(8,128)(2,1)} async-done(((bf16[4,256,2048]{2,1,0:T(8,128)(2,1)}), bf16[4,256,2048]{2,1,0:T(8,128)(2,1)}, u32[]{:S(2)}, u32[]{:S(2)}) %all-to-all-start.3) | async-done | bytes 4194336 | tf_op jit(solution)/shard_map/all_to_all | solution.py:381
  354.8 4.7 all-to-all-start.4
  363.8 3.1 reduce_sum.82
  369.9 25.8 %all-to-all-done.4 = bf16[4,256,1536]{2,1,0:T(8,128)(2,1)} async-done(((bf16[4,256,1536]{2,1,0:T(8,128)(2,1)}), bf16[4,256,1536]{2,1,0:T(8,128)(2,1)}, u32[]{:S(2)}, u32[]{:S(2)}) %all-to-all-start.4) | async-done | bytes 3145760 | tf_op jit(solution)/shard_map/all_to_all | solution.py:381
  399.9 4.5 all-to-all-start.5
  410.0 5.9 %collective-permute-done.17 = bf16[64,2048]{1,0:T(8,128)(2,1)S(1)} collective-permute-done((bf16[64,2048]{1,0:T(8,128)(2,1)}, bf16[64,2048]{1,0:T(8,128)(2,1)S(1)}, u32[]{:S(2)}, u32[]{:S(2)}) %collective-permute-start.17) | collective-permute-done | bytes 262176 | tf_op jit(solution)/shard_map/ppermute | solution.py:386
  415.9 4.2 collective-permute-done.19
  431.7 21.1 %all-to-all-done.5.in_ref = bf16[4,64,3584]{2,1,0:T(8,128)(2,1)S(1)} async-done(((bf16[4,64,3584]{2,1,0:T(8,128)(2,1)}), bf16[4,64,3584]{2,1,0:T(8,128)(2,1)S(1)}, u32[]{:S(2)}, u32[]{:S(2)}) %all-to-all-start.5) | async-done | bytes 1835040 | tf_op jit(solution)/shard_map/all_to_all | solution.py:381
  453.7 9.8 %all-to-all-start.6 = ((f32[32,1,768]{2,1,0:T(1,128)}), f32[32,1,768]{2,1,0:T(1,128)S(1)}, u32[]{:S(2)}, u32[]{:S(2)}) async-start(f32[32,1,768]{2,1,0:T(1,128)} %copy.63), calls=%async_computation.8 | async-start | bytes 196608 | tf_op jit(solution)/shard_map/all_to_all | solution.py:381
  463.5 3.3 fusion.8
  (222 shorter events, 106.1 us)
Async XLA Ops:
  10.1 59.6 %all-to-all-start = ((bf16[4,64,3584]{2,1,0:T(8,128)(2,1)}), bf16[4,64,3584]{2,1,0:T(8,128)(2,1)S(1)}, u32[]{:S(2)}, u32[]{:S(2)}) async-start(bf16[4,64,3584]{2,1,0:T(8,128)(2,1)} %shard_map.263), calls=%async_computation | async-start | bytes 3670016 | tf_op jit(solution)/shard_map/all_to_all | solution.py:381
  16.6 169.7 %all-gather.3.cloned.1.call-start = ((), (), s32[]{:S(2)}) async-start(), calls=%async_computation.13 | async-start | bytes 20054016 | tf_op jit(solution)/shard_map/all_gather | solution.py:487
  17.5 45.3 %collective-permute-start.1 = (bf16[16,1536]{1,0:T(8,128)(2,1)S(1)}, bf16[16,1536]{1,0:T(8,128)(2,1)S(1)}, u32[]{:S(2)}, u32[]{:S(2)}) collective-permute-start(bf16[16,1536]{1,0:T(8,128)(2,1)S(1)} %broadcast_in_dim.122), channel_id=1, source_target_pairs={{0,2},{1,3},{2,0},{3,1},{4,6},{5,7},{6,4},{7,5},{8,10},{9,11},{10,... | collective-permute-start | bytes 147464 | tf_op jit(solution)/shard_map/ppermute | solution.py:391
  20.5 42.8 %collective-permute-start = (bf16[16,1536]{1,0:T(8,128)(2,1)S(1)}, bf16[16,1536]{1,0:T(8,128)(2,1)S(1)}, u32[]{:S(2)}, u32[]{:S(2)}) collective-permute-start(bf16[16,1536]{1,0:T(8,128)(2,1)S(1)} %broadcast_in_dim.122), channel_id=1, source_target_pairs={{0,1},{1,2},{2,3},{3,0},{4,5},{5,6},{6,7},{7,4},{8,9},{9,10},{10,1... | collective-permute-start | bytes 147464 | tf_op jit(solution)/shard_map/ppermute | solution.py:391
  21.9 45.2 %collective-permute-start.5 = (bf16[256,2048]{1,0:T(8,128)(2,1)}, bf16[256,2048]{1,0:T(8,128)(2,1)}, u32[]{:S(2)}, u32[]{:S(2)}) collective-permute-start(bf16[256,2048]{1,0:T(8,128)(2,1)} %refs_9_), channel_id=1, source_target_pairs={{0,16},{8,24},{16,0},{24,8},{1,17},{9,25},{17,1},{25,9},{2,18},{10... | collective-permute-start | bytes 3145736 | tf_op jit(solution)/shard_map/ppermute | solution.py:386
  23.4 43.7 %collective-permute-start.4 = (bf16[256,2048]{1,0:T(8,128)(2,1)}, bf16[256,2048]{1,0:T(8,128)(2,1)}, u32[]{:S(2)}, u32[]{:S(2)}) collective-permute-start(bf16[256,2048]{1,0:T(8,128)(2,1)} %refs_9_), channel_id=1, source_target_pairs={{0,8},{8,0},{16,24},{24,16},{1,9},{9,1},{17,25},{25,17},{2,10},{10... | collective-permute-start | bytes 3145736 | tf_op jit(solution)/shard_map/ppermute | solution.py:386
  24.9 44.7 %collective-permute-start.6 = (bf16[256,2048]{1,0:T(8,128)(2,1)}, bf16[256,2048]{1,0:T(8,128)(2,1)}, u32[]{:S(2)}, u32[]{:S(2)}) collective-permute-start(bf16[256,2048]{1,0:T(8,128)(2,1)} %refs_9_), channel_id=1, source_target_pairs={{0,24},{8,16},{16,8},{24,0},{1,25},{9,17},{17,9},{25,1},{2,26},{10... | collective-permute-start | bytes 3145736 | tf_op jit(solution)/shard_map/ppermute | solution.py:386
  62.8 4.1 collective-permute-start.2
  63.2 3.8 collective-permute-start.3
  76.3 37.7 %collective-permute-start.7 = (bf16[128,4096]{1,0:T(8,128)(2,1)S(1)}, bf16[128,4096]{1,0:T(8,128)(2,1)S(1)}, u32[]{:S(2)}, u32[]{:S(2)}) collective-permute-start(bf16[128,4096]{1,0:T(8,128)(2,1)S(1)} %copy-done.5), channel_id=1, source_target_pairs={{0,1},{1,2},{2,3},{3,0},{4,5},{5,6},{6,7},{7,4},{8,9},{9,10},{10,1... | collective-permute-start | bytes 3145736 | tf_op jit(solution)/shard_map/ppermute | solution.py:391
  90.5 91.9 %collective-permute-start.9 = (bf16[128,4096]{1,0:T(8,128)(2,1)S(1)}, bf16[128,4096]{1,0:T(8,128)(2,1)S(1)}, u32[]{:S(2)}, u32[]{:S(2)}) collective-permute-start(bf16[128,4096]{1,0:T(8,128)(2,1)S(1)} %copy-done.5), channel_id=1, source_target_pairs={{0,3},{1,0},{2,1},{3,2},{4,7},{5,4},{6,5},{7,6},{8,11},{9,8},{10,9... | collective-permute-start | bytes 3145736 | tf_op jit(solution)/shard_map/ppermute | solution.py:391
  90.5 90.8 %collective-permute-start.8 = (bf16[128,4096]{1,0:T(8,128)(2,1)S(1)}, bf16[128,4096]{1,0:T(8,128)(2,1)S(1)}, u32[]{:S(2)}, u32[]{:S(2)}) collective-permute-start(bf16[128,4096]{1,0:T(8,128)(2,1)S(1)} %copy-done.5), channel_id=1, source_target_pairs={{0,2},{1,3},{2,0},{3,1},{4,6},{5,7},{6,4},{7,5},{8,10},{9,11},{10,... | collective-permute-start | bytes 3145736 | tf_op jit(solution)/shard_map/ppermute | solution.py:391
  91.9 91.4 %collective-permute-start.10 = (bf16[256,2048]{1,0:T(8,128)(2,1)S(1)}, bf16[256,2048]{1,0:T(8,128)(2,1)S(1)}, u32[]{:S(2)}, u32[]{:S(2)}) collective-permute-start(bf16[256,2048]{1,0:T(8,128)(2,1)S(1)} %copy-done.12), channel_id=1, source_target_pairs={{0,4},{4,0},{1,5},{5,1},{2,6},{6,2},{3,7},{7,3},{8,12},{12,8},{9,1... | collective-permute-start | bytes 3145736 | tf_op jit(solution)/shard_map/ppermute | solution.py:377
  93.9 90.4 %collective-permute-start.11 = (bf16[256,2048]{1,0:T(8,128)(2,1)}, bf16[256,2048]{1,0:T(8,128)(2,1)S(1)}, u32[]{:S(2)}, u32[]{:S(2)}) collective-permute-start(bf16[256,2048]{1,0:T(8,128)(2,1)} %collective-permute-done.4.refs_10_), channel_id=1, source_target_pairs={{0,4},{4,0},{1,5},{5,1},{2,6},{6,2},{3,7},{7,3},{8,12},{12,8},{9,1... | collective-permute-start | bytes 3145736 | tf_op jit(solution)/shard_map/ppermute | solution.py:377
  113.9 71.4 %collective-permute-start.12 = (bf16[256,2048]{1,0:T(8,128)(2,1)}, bf16[256,2048]{1,0:T(8,128)(2,1)S(1)}, u32[]{:S(2)}, u32[]{:S(2)}) collective-permute-start(bf16[256,2048]{1,0:T(8,128)(2,1)} %collective-permute-done.5.refs_11_), channel_id=1, source_target_pairs={{0,4},{4,0},{1,5},{5,1},{2,6},{6,2},{3,7},{7,3},{8,12},{12,8},{9,1... | collective-permute-start | bytes 3145736 | tf_op jit(solution)/shard_map/ppermute | solution.py:377
  181.3 5.0 %collective-permute-start.13 = (bf16[256,2048]{1,0:T(8,128)(2,1)}, bf16[256,2048]{1,0:T(8,128)(2,1)}, u32[]{:S(2)}, u32[]{:S(2)}) collective-permute-start(bf16[256,2048]{1,0:T(8,128)(2,1)} %collective-permute-done.6.refs_12_), channel_id=1, source_target_pairs={{0,4},{4,0},{1,5},{5,1},{2,6},{6,2},{3,7},{7,3},{8,12},{12,8},{9,1... | collective-permute-start | bytes 3145736 | tf_op jit(solution)/shard_map/ppermute | solution.py:377
  204.4 36.6 %all-to-all-start.1 = ((bf16[8,128,1024]{2,1,0:T(8,128)(2,1)}), bf16[8,128,1024]{2,1,0:T(8,128)(2,1)S(1)}, u32[]{:S(2)}, u32[]{:S(2)}) async-start(bf16[8,128,1024]{2,1,0:T(8,128)(2,1)} %bitcast.135), calls=%async_computation.1 | async-start | bytes 4194304 | tf_op jit(solution)/shard_map/all_to_all | solution.py:381
  256.4 7.6 %collective-permute-start.14 = (bf16[1024,2048]{1,0:T(8,128)(2,1)}, bf16[1024,2048]{1,0:T(8,128)(2,1)}, u32[]{:S(2)}, u32[]{:S(2)}) collective-permute-start(bf16[1024,2048]{1,0:T(8,128)(2,1)} %convolution_convert_fusion.2), channel_id=1, source_target_pairs={{0,4},{4,0},{1,5},{5,1},{2,6},{6,2},{3,7},{7,3},{8,12},{12,8},{9,1... | collective-permute-start | bytes 12582920 | tf_op jit(solution)/shard_map/ppermute | solution.py:377
  256.9 30.5 %all-to-all-start.2 = ((bf16[8,128,1024]{2,1,0:T(8,128)(2,1)}), bf16[8,128,1024]{2,1,0:T(8,128)(2,1)S(1)}, u32[]{:S(2)}, u32[]{:S(2)}) async-start(bf16[8,128,1024]{2,1,0:T(8,128)(2,1)} %bitcast.28), calls=%async_computation.2 | async-start | bytes 4194304 | tf_op jit(solution)/shard_map/all_to_all | solution.py:381
  260.7 83.6 %reduce-scatter.4.cloned.1.call-start = ((), (), s32[]{:S(2)}) async-start(), calls=%async_computation.10 | async-start | bytes 2621440 | tf_op jit(solution)/shard_map/reduce_scatter | solution.py:535
  301.3 6.1 %collective-permute-start.15 = (bf16[1024,1536]{1,0:T(8,128)(2,1)}, bf16[1024,1536]{1,0:T(8,128)(2,1)}, u32[]{:S(2)}, u32[]{:S(2)}) collective-permute-start(bf16[1024,1536]{1,0:T(8,128)(2,1)} %convolution_convert_fusion.1), channel_id=1, source_target_pairs={{0,4},{4,0},{1,5},{5,1},{2,6},{6,2},{3,7},{7,3},{8,12},{12,8},{9,1... | collective-permute-start | bytes 9437192 | tf_op jit(solution)/shard_map/ppermute | solution.py:377
  301.4 53.3 %all-to-all-start.3 = ((bf16[4,256,2048]{2,1,0:T(8,128)(2,1)}), bf16[4,256,2048]{2,1,0:T(8,128)(2,1)}, u32[]{:S(2)}, u32[]{:S(2)}) async-start(bf16[4,256,2048]{2,1,0:T(8,128)(2,1)} %bitcast.131), calls=%async_computation.5 | async-start | bytes 8388608 | tf_op jit(solution)/shard_map/all_to_all | solution.py:381
  306.5 123.7 %reduce-scatter.6.cloned.1.call-start = ((), (), s32[]{:S(2)}) async-start(), calls=%async_computation.11 | async-start | bytes 2621440 | tf_op jit(solution)/shard_map/reduce_scatter | solution.py:542
  354.8 41.0 %all-to-all-start.4 = ((bf16[4,256,1536]{2,1,0:T(8,128)(2,1)}), bf16[4,256,1536]{2,1,0:T(8,128)(2,1)}, u32[]{:S(2)}, u32[]{:S(2)}) async-start(bf16[4,256,1536]{2,1,0:T(8,128)(2,1)} %bitcast.132), calls=%async_computation.6 | async-start | bytes 6291456 | tf_op jit(solution)/shard_map/all_to_all | solution.py:381
  359.4 115.0 %reduce-scatter.8.cloned.1.call-start = ((), (), s32[]{:S(2)}) async-start(), calls=%async_computation.12 | async-start | bytes 9437184 | tf_op jit(solution)/shard_map/reduce_scatter | solution.py:550
  363.7 3.2 collective-permute-start.16
  399.9 52.9 %all-to-all-start.5 = ((bf16[4,64,3584]{2,1,0:T(8,128)(2,1)}), bf16[4,64,3584]{2,1,0:T(8,128)(2,1)S(1)}, u32[]{:S(2)}, u32[]{:S(2)}) async-start(bf16[4,64,3584]{2,1,0:T(8,128)(2,1)} %bitcast.128), calls=%async_computation.7 | async-start | bytes 3670016 | tf_op jit(solution)/shard_map/all_to_all | solution.py:381
  406.4 9.5 %collective-permute-start.17 = (bf16[64,2048]{1,0:T(8,128)(2,1)}, bf16[64,2048]{1,0:T(8,128)(2,1)S(1)}, u32[]{:S(2)}, u32[]{:S(2)}) collective-permute-start(bf16[64,2048]{1,0:T(8,128)(2,1)} %get-tuple-element.124), channel_id=1, source_target_pairs={{0,8},{8,0},{16,24},{24,16},{1,9},{9,1},{17,25},{25,17},{2,10},{10... | collective-permute-start | bytes 786440 | tf_op jit(solution)/shard_map/ppermute | solution.py:386
  407.9 12.1 %collective-permute-start.19 = (bf16[64,2048]{1,0:T(8,128)(2,1)}, bf16[64,2048]{1,0:T(8,128)(2,1)}, u32[]{:S(2)}, u32[]{:S(2)}) collective-permute-start(bf16[64,2048]{1,0:T(8,128)(2,1)} %get-tuple-element.125), channel_id=1, source_target_pairs={{0,24},{8,16},{16,8},{24,0},{1,25},{9,17},{17,9},{25,1},{2,26},{10... | collective-permute-start | bytes 786440 | tf_op jit(solution)/shard_map/ppermute | solution.py:386
  409.5 11.7 %collective-permute-start.18 = (bf16[64,2048]{1,0:T(8,128)(2,1)S(1)}, bf16[64,2048]{1,0:T(8,128)(2,1)}, u32[]{:S(2)}, u32[]{:S(2)}) collective-permute-start(bf16[64,2048]{1,0:T(8,128)(2,1)S(1)} %get-tuple-element.126), channel_id=1, source_target_pairs={{0,16},{8,24},{16,0},{24,8},{1,17},{9,25},{17,1},{25,9},{2,18},{10... | collective-permute-start | bytes 786440 | tf_op jit(solution)/shard_map/ppermute | solution.py:386
  422.5 5.9 %collective-permute-start.20 = (bf16[64,2048]{1,0:T(8,128)(2,1)S(1)}, bf16[64,2048]{1,0:T(8,128)(2,1)}, u32[]{:S(2)}, u32[]{:S(2)}) collective-permute-start(bf16[64,2048]{1,0:T(8,128)(2,1)S(1)} %fusion.27), channel_id=1, source_target_pairs={{0,0},{4,1},{8,2},{12,3},{16,4},{20,5},{24,6},{28,7},{1,8},{5,9},{... | collective-permute-start | bytes 786440 | tf_op jit(solution)/shard_map/ppermute | solution.py:552
  453.7 19.0 %all-to-all-start.6 = ((f32[32,1,768]{2,1,0:T(1,128)}), f32[32,1,768]{2,1,0:T(1,128)S(1)}, u32[]{:S(2)}, u32[]{:S(2)}) async-start(f32[32,1,768]{2,1,0:T(1,128)} %copy.63), calls=%async_computation.8 | async-start | bytes 196608 | tf_op jit(solution)/shard_map/all_to_all | solution.py:381
  (34 other events, 366.4 us)
Sparse Core Ops, SparseCore 0:
  75.2 109.3 all-gather.2
  301.5 42.8 reduce-scatter.3
  347.3 43.1 reduce-scatter.5
  395.9 77.6 reduce-scatter.7
